TPU v7x, 32 devices: a whole 2x2x4 slice. The times are simulated.
32 devices in a mesh: seq: 8 (over z, x), fsdp: 4 (over y, core).
Axes of the slice: x: 2, y: 2, z: 4, core: 2. Of those that a mesh axis runs over, the one named last changes fastest.
Arguments:
- tokens: bfloat16 [4096, 1536], P(('seq', 'fsdp')), may hold values from -6 to 6
- cotangent: bfloat16 [4096, 1536], P(('seq', 'fsdp')), may hold values from -6 to 6
- lengths: int32 [7], replicated, may hold values from 1 to 3585, 4096 in all
- attn_gain: bfloat16 [1536], P(('seq', 'fsdp')), may hold values from 0.5 to 1.5
- q_weight: bfloat16 [1536, 1536], P(('seq', 'fsdp')), may hold values from -0.15625 to 0.15625
- q_bias: bfloat16 [1536], P(('seq', 'fsdp')), may hold values from -3 to 3
- k_weight: bfloat16 [1536, 256], P(('seq', 'fsdp')), may hold values from -0.15625 to 0.15625
- k_bias: bfloat16 [256], P(('seq', 'fsdp')), may hold values from -3 to 3
- v_weight: bfloat16 [1536, 256], P(('seq', 'fsdp')), may hold values from -0.15625 to 0.15625
- v_bias: bfloat16 [256], P(('seq', 'fsdp')), may hold values from -3 to 3
- o_weight: bfloat16 [1536, 1536], P(('seq', 'fsdp')), may hold values from -1.25 to 1.25
- mlp_gain: bfloat16 [1536], P(('seq', 'fsdp')), may hold values from 0.5 to 1.5
- gate_weight: bfloat16 [1536, 8960], P(('seq', 'fsdp')), may hold values from -0.15625 to 0.15625
- up_weight: bfloat16 [1536, 8960], P(('seq', 'fsdp')), may hold values from -0.15625 to 0.15625
- down_weight: bfloat16 [8960, 1536], P(('seq', 'fsdp')), may hold values from -0.0625 to 0.0625
Outputs:
- layer_out: bfloat16 [4096, 1536], P(('seq', 'fsdp'))
- input_grad: float32 [4096, 1536], P(('seq', 'fsdp'))
- attn_gain_grad: float32 [1536], P(('seq', 'fsdp'))
- q_weight_grad: float32 [1536, 1536], P(('seq', 'fsdp'))
- q_bias_grad: float32 [1536], P(('seq', 'fsdp'))
- k_weight_grad: float32 [1536, 256], P(('seq', 'fsdp'))
- k_bias_grad: float32 [256], P(('seq', 'fsdp'))
- v_weight_grad: float32 [1536, 256], P(('seq', 'fsdp'))
- v_bias_grad: float32 [256], P(('seq', 'fsdp'))
- o_weight_grad: float32 [1536, 1536], P(('seq', 'fsdp'))
- mlp_gain_grad: float32 [1536], P(('seq', 'fsdp'))
- gate_weight_grad: float32 [1536, 8960], P(('seq', 'fsdp'))
- up_weight_grad: float32 [1536, 8960], P(('seq', 'fsdp'))
- down_weight_grad: float32 [8960, 1536], P(('seq', 'fsdp'))
Inputs may be any that keep to these rules, and one draw needn't show every extreme that they name: The lengths of the 7 packed sequences in order; they sum to 4096 and the longest has exactly 3585 tokens.
All inputs are finite; a program needn't handle non-finite values.
Results may differ from a plain program's by a relative error of at most 0.02.
Values may be sent and summed in bfloat16 or wider, within the bound.
A program may use at most 896 MiB of HBM per device.

v0:
```python
import jax
import jax.numpy as jnp
from jax import lax
from jax.sharding import PartitionSpec as P

HEADS = 12
KV_HEADS = 2
HEAD_DIM = 128


EPSILON = 1e-06
ROPE_BASE = 10000.0


def segment_of(positions, lengths):
    seg_ends = jnp.cumsum(lengths)
    seg_starts = seg_ends - lengths
    inside = (positions[:, None] >= seg_starts[None, :]) & (positions[:, None] < seg_ends[None, :])
    labels = jnp.arange(lengths.shape[0], dtype=jnp.int32)
    segment = jnp.sum(jnp.where(inside, labels[None, :], 0), axis=1)
    seg_begin = jnp.sum(jnp.where(inside, seg_starts[None, :], 0), axis=1)
    return (segment, positions - seg_begin, seg_begin)


def rope_tables(places, head_size):
    half_size = head_size // 2
    frequency = ROPE_BASE ** (-2.0 * jnp.arange(half_size, dtype=jnp.float32) / head_size)
    angles = places.astype(jnp.float32)[:, None] * frequency[None, :]
    return (jnp.cos(angles), jnp.sin(angles))


def rotate(vector, cosine, sine_table, direction):
    half_size = vector.shape[-1] // 2
    front_half = vector[..., :half_size]
    back_half = vector[..., half_size:]
    cosine = cosine[:, None, :]
    sine_table = direction * sine_table[:, None, :]
    return jnp.concatenate(
        [
            front_half * cosine - back_half * sine_table,
            back_half * cosine + front_half * sine_table,
        ],
        axis=-1,
    )


def keep_state(state):
    return state


def norm_back(grad_normed, normed, inverse, gain_row):
    scaled = grad_normed * gain_row.astype(jnp.float32)
    return inverse * (scaled - normed * jnp.mean(scaled * normed, axis=-1, keepdims=True))


def shards(
    tokens,
    cotangent,
    lengths,
    attn_gain,
    q_weight,
    q_bias,
    k_weight,
    k_bias,
    v_weight,
    v_bias,
    o_weight,
    mlp_gain,
    gate_weight,
    up_weight,
    down_weight,
):
    local_rows = tokens.shape[0]
    group_size = HEADS // KV_HEADS
    key_width = KV_HEADS * HEAD_DIM
    device_count = lax.axis_size(("seq", "fsdp"))
    total_rows = local_rows * device_count
    first_row = lax.axis_index(("seq", "fsdp")) * local_rows
    local_positions = first_row + jnp.arange(local_rows, dtype=jnp.int32)
    query_segment, query_places, query_begin = segment_of(local_positions, lengths)
    cosine, sine_table = rope_tables(query_places, HEAD_DIM)
    score_scale = HEAD_DIM ** (-0.5)
    key_span = local_rows * min(max(1, 1024 // local_rows), device_count)
    key_blocks = total_rows // key_span
    reach_low = query_begin[0]
    reach_high = first_row + local_rows - 1
    gain_one, w_query, b_query, w_key, b_key, w_value, b_value, w_out = (
        lax.all_gather(attn_gain, ("seq", "fsdp"), axis=0, tiled=True),
        lax.all_gather(q_weight, ("seq", "fsdp"), axis=0, tiled=True),
        lax.all_gather(q_bias, ("seq", "fsdp"), axis=0, tiled=True),
        lax.all_gather(k_weight, ("seq", "fsdp"), axis=0, tiled=True),
        lax.all_gather(k_bias, ("seq", "fsdp"), axis=0, tiled=True),
        lax.all_gather(v_weight, ("seq", "fsdp"), axis=0, tiled=True),
        lax.all_gather(v_bias, ("seq", "fsdp"), axis=0, tiled=True),
        lax.all_gather(o_weight, ("seq", "fsdp"), axis=0, tiled=True),
    )
    inputs = tokens.astype(jnp.float32)
    inv_one = lax.rsqrt(jnp.mean(inputs * inputs, axis=-1, keepdims=True) + EPSILON)
    normed_one = inputs * inv_one
    hidden_one = (normed_one * gain_one.astype(jnp.float32)).astype(jnp.bfloat16)
    query_lin = jnp.dot(hidden_one, w_query, preferred_element_type=jnp.float32) + b_query.astype(
        jnp.float32
    )
    key_lin = jnp.dot(hidden_one, w_key, preferred_element_type=jnp.float32) + b_key.astype(
        jnp.float32
    )
    value_lin = jnp.dot(hidden_one, w_value, preferred_element_type=jnp.float32) + b_value.astype(
        jnp.float32
    )
    queries = rotate(
        query_lin.reshape(local_rows, HEADS, HEAD_DIM), cosine, sine_table, 1.0
    ).astype(jnp.bfloat16)
    queries = queries.reshape(local_rows, KV_HEADS, group_size, HEAD_DIM)
    keys_flat = (
        rotate(key_lin.reshape(local_rows, KV_HEADS, HEAD_DIM), cosine, sine_table, 1.0)
        .astype(jnp.bfloat16)
        .reshape(local_rows, key_width)
    )
    values_flat = value_lin.astype(jnp.bfloat16)
    all_keys, all_values = (
        lax.all_gather(keys_flat, ("seq", "fsdp"), axis=0, tiled=True),
        lax.all_gather(values_flat, ("seq", "fsdp"), axis=0, tiled=True),
    )

    def needed(key_base):
        return (key_base <= reach_high) & (key_base + key_span - 1 >= reach_low)

    def visible_at(key_base):
        key_positions = key_base + jnp.arange(key_span, dtype=jnp.int32)
        key_segment, key_places, key_begin = segment_of(key_positions, lengths)
        return (query_segment[:, None] == key_segment[None, :]) & (
            local_positions[:, None] >= key_positions[None, :]
        )

    def key_slice(stacked, key_base):
        return lax.dynamic_slice_in_dim(stacked, key_base, key_span, 0).reshape(
            key_span, KV_HEADS, HEAD_DIM
        )

    def scores_at(stacked_keys, key_base):
        key_rows = key_slice(stacked_keys, key_base)
        raw_scores = jnp.einsum(
            "tgjd,kgd->gjtk", queries, key_rows, preferred_element_type=jnp.float32
        )
        return (raw_scores * score_scale, key_rows)

    def max_step(number, state_in):
        key_base = number * key_span

        def max_compute_block(state):
            running_max, running_sum = state
            scaled, key_rows = scores_at(all_keys, key_base)
            visible = visible_at(key_base)
            masked = jnp.where(visible, scaled, -1e30)
            new_max = jnp.maximum(running_max, jnp.max(masked, axis=-1))
            weights = jnp.where(visible, jnp.exp(masked - new_max[..., None]), 0.0)
            return (
                new_max,
                running_sum * jnp.exp(running_max - new_max) + jnp.sum(weights, axis=-1),
            )

        return lax.cond(needed(key_base), max_compute_block, keep_state, state_in)

    start_max = jnp.full((KV_HEADS, group_size, local_rows), -1e30, jnp.float32)
    start_sum = jnp.zeros((KV_HEADS, group_size, local_rows), jnp.float32)
    running_max, running_sum = lax.fori_loop(0, key_blocks, max_step, (start_max, start_sum))
    log_mass = running_max + jnp.log(running_sum)

    def probs_at(stacked_keys, key_base):
        scaled, key_rows = scores_at(stacked_keys, key_base)
        return (
            jnp.where(visible_at(key_base), jnp.exp(scaled - log_mass[..., None]), 0.0),
            key_rows,
        )

    def mix_step(number, mixed_acc):
        key_base = number * key_span

        def mix_compute_block(accumulated):
            attn_probs, key_rows = probs_at(all_keys, key_base)
            value_rows = key_slice(all_values, key_base)
            return accumulated + jnp.einsum(
                "gjtk,kgd->tgjd",
                attn_probs.astype(jnp.bfloat16),
                value_rows,
                preferred_element_type=jnp.float32,
            )

        return lax.cond(needed(key_base), mix_compute_block, keep_state, mixed_acc)

    mixed_sum = lax.fori_loop(
        0,
        key_blocks,
        mix_step,
        jnp.zeros((local_rows, KV_HEADS, group_size, HEAD_DIM), jnp.float32),
    )
    mixed_low = mixed_sum.reshape(local_rows, HEADS * HEAD_DIM).astype(jnp.bfloat16)
    middle = inputs + jnp.dot(mixed_low, w_out, preferred_element_type=jnp.float32)
    inv_two = lax.rsqrt(jnp.mean(middle * middle, axis=-1, keepdims=True) + EPSILON)
    normed_two = middle * inv_two
    grad_out = cotangent.astype(jnp.float32)
    gain_two, w_gate, w_up, w_down = (
        lax.all_gather(mlp_gain, ("seq", "fsdp"), axis=0, tiled=True),
        lax.all_gather(gate_weight, ("seq", "fsdp"), axis=0, tiled=True),
        lax.all_gather(up_weight, ("seq", "fsdp"), axis=0, tiled=True),
        lax.all_gather(down_weight, ("seq", "fsdp"), axis=0, tiled=True),
    )
    hidden_two = (normed_two * gain_two.astype(jnp.float32)).astype(jnp.bfloat16)
    gate_act = jnp.dot(hidden_two, w_gate, preferred_element_type=jnp.float32)
    up_act = jnp.dot(hidden_two, w_up, preferred_element_type=jnp.float32)
    sigma = jax.nn.sigmoid(gate_act)
    silu_act = gate_act * sigma
    activated = (silu_act * up_act).astype(jnp.bfloat16)
    result = middle + jnp.dot(activated, w_down, preferred_element_type=jnp.float32)
    layer_out = result.astype(jnp.bfloat16)
    gain_two, w_gate, w_up, w_down = (
        lax.all_gather(mlp_gain, ("seq", "fsdp"), axis=0, tiled=True),
        lax.all_gather(gate_weight, ("seq", "fsdp"), axis=0, tiled=True),
        lax.all_gather(up_weight, ("seq", "fsdp"), axis=0, tiled=True),
        lax.all_gather(down_weight, ("seq", "fsdp"), axis=0, tiled=True),
    )
    grad_activ = jnp.dot(cotangent, w_down.T, preferred_element_type=jnp.float32)
    grad_gate = (grad_activ * up_act * sigma * (1.0 + gate_act * (1.0 - sigma))).astype(
        jnp.bfloat16
    )
    grad_up = (grad_activ * silu_act).astype(jnp.bfloat16)
    grad_hidden_two = jnp.dot(grad_gate, w_gate.T, preferred_element_type=jnp.float32) + jnp.dot(
        grad_up, w_up.T, preferred_element_type=jnp.float32
    )
    gain_two_grad = jnp.sum(grad_hidden_two * normed_two, axis=0)
    grad_middle = grad_out + norm_back(grad_hidden_two, normed_two, inv_two, gain_two)
    gain_one, w_query, w_key, w_value, w_out = (
        lax.all_gather(attn_gain, ("seq", "fsdp"), axis=0, tiled=True),
        lax.all_gather(q_weight, ("seq", "fsdp"), axis=0, tiled=True),
        lax.all_gather(k_weight, ("seq", "fsdp"), axis=0, tiled=True),
        lax.all_gather(v_weight, ("seq", "fsdp"), axis=0, tiled=True),
        lax.all_gather(o_weight, ("seq", "fsdp"), axis=0, tiled=True),
    )
    grad_branch = grad_middle.astype(jnp.bfloat16)
    grad_mixed = jnp.dot(grad_branch, w_out.T, preferred_element_type=jnp.float32).astype(
        jnp.bfloat16
    )
    grad_mixed = grad_mixed.reshape(local_rows, KV_HEADS, group_size, HEAD_DIM)
    back_keys, back_values = (all_keys, all_values)

    def delta_step(number, delta_acc):
        key_base = number * key_span

        def delta_compute_block(accumulated):
            attn_probs, key_rows = probs_at(back_keys, key_base)
            value_rows = key_slice(back_values, key_base)
            grad_probs = jnp.einsum(
                "tgjd,kgd->gjtk", grad_mixed, value_rows, preferred_element_type=jnp.float32
            )
            return accumulated + jnp.sum(attn_probs * grad_probs, axis=-1)

        return lax.cond(needed(key_base), delta_compute_block, keep_state, delta_acc)

    delta = lax.fori_loop(
        0, key_blocks, delta_step, jnp.zeros((KV_HEADS, group_size, local_rows), jnp.float32)
    )

    def grad_step(number, state_in):
        key_base = number * key_span

        def grad_compute_block(state):
            query_acc, key_part, value_part = state
            attn_probs, key_rows = probs_at(back_keys, key_base)
            value_rows = key_slice(back_values, key_base)
            grad_probs = jnp.einsum(
                "tgjd,kgd->gjtk", grad_mixed, value_rows, preferred_element_type=jnp.float32
            )
            grad_scores = (attn_probs * (grad_probs - delta[..., None])).astype(jnp.bfloat16)
            query_acc = query_acc + jnp.einsum(
                "gjtk,kgd->tgjd", grad_scores, key_rows, preferred_element_type=jnp.float32
            )
            key_block = jnp.einsum(
                "gjtk,tgjd->kgd", grad_scores, queries, preferred_element_type=jnp.float32
            ).reshape(key_span, key_width)
            value_block = jnp.einsum(
                "gjtk,tgjd->kgd",
                attn_probs.astype(jnp.bfloat16),
                grad_mixed,
                preferred_element_type=jnp.float32,
            ).reshape(key_span, key_width)
            key_part = lax.dynamic_update_slice_in_dim(key_part, key_block, key_base, 0)
            value_part = lax.dynamic_update_slice_in_dim(value_part, value_block, key_base, 0)
            return (query_acc, key_part, value_part)

        return lax.cond(needed(key_base), grad_compute_block, keep_state, state_in)

    start_query = jnp.zeros((local_rows, KV_HEADS, group_size, HEAD_DIM), jnp.float32)
    start_part = jnp.zeros((total_rows, key_width), jnp.float32)
    query_acc, key_part, value_part = lax.fori_loop(
        0, key_blocks, grad_step, (start_query, start_part, start_part)
    )
    key_sum, value_sum = (
        lax.psum_scatter(key_part, ("seq", "fsdp"), scatter_dimension=0, tiled=True),
        lax.psum_scatter(value_part, ("seq", "fsdp"), scatter_dimension=0, tiled=True),
    )
    grad_query = rotate(
        query_acc.reshape(local_rows, HEADS, HEAD_DIM) * score_scale, cosine, sine_table, -1.0
    )
    grad_query = grad_query.reshape(local_rows, HEADS * HEAD_DIM).astype(jnp.bfloat16)
    grad_key = rotate(
        key_sum.reshape(local_rows, KV_HEADS, HEAD_DIM) * score_scale, cosine, sine_table, -1.0
    )
    grad_key = grad_key.reshape(local_rows, key_width).astype(jnp.bfloat16)
    grad_value = value_sum.astype(jnp.bfloat16)
    query_b_grad = jnp.sum(grad_query.astype(jnp.float32), axis=0)
    key_b_grad = jnp.sum(grad_key.astype(jnp.float32), axis=0)
    value_b_grad = jnp.sum(grad_value.astype(jnp.float32), axis=0)
    grad_hidden_one = jnp.dot(grad_query, w_query.T, preferred_element_type=jnp.float32)
    grad_hidden_one = grad_hidden_one + jnp.dot(
        grad_key, w_key.T, preferred_element_type=jnp.float32
    )
    grad_hidden_one = grad_hidden_one + jnp.dot(
        grad_value, w_value.T, preferred_element_type=jnp.float32
    )
    gain_one_grad = jnp.sum(grad_hidden_one * normed_one, axis=0)
    input_grad = grad_middle + norm_back(grad_hidden_one, normed_one, inv_one, gain_one)
    query_cols = grad_query.shape[1]
    ff_cols = grad_gate.shape[1]
    first_part = hidden_one.T
    second_part = hidden_two.T
    row_sums = lax.psum_scatter(
        jnp.concatenate(
            [
                jnp.dot(first_part, grad_query, preferred_element_type=jnp.float32),
                jnp.dot(first_part, grad_key, preferred_element_type=jnp.float32),
                jnp.dot(first_part, grad_value, preferred_element_type=jnp.float32),
                jnp.dot(second_part, grad_gate, preferred_element_type=jnp.float32),
                jnp.dot(second_part, grad_up, preferred_element_type=jnp.float32),
            ],
            axis=1,
        ),
        ("seq", "fsdp"),
        scatter_dimension=0,
        tiled=True,
    )
    query_w_grad = row_sums[:, :query_cols]
    key_w_grad = row_sums[:, query_cols : query_cols + key_width]
    value_w_grad = row_sums[:, query_cols + key_width : query_cols + 2 * key_width]
    gate_final = row_sums[:, query_cols + 2 * key_width : query_cols + 2 * key_width + ff_cols]
    up_final = row_sums[:, query_cols + 2 * key_width + ff_cols :]
    query_share = query_cols // device_count
    ff_share = ff_cols // device_count
    share_rows = query_share + ff_share
    model_width = grad_branch.shape[1]
    owners = share_rows * lax.axis_size(("seq", "fsdp")) // share_rows
    out_term = jnp.dot(mixed_low.T, grad_branch, preferred_element_type=jnp.float32).reshape(
        owners, query_share, model_width
    )
    down_term = jnp.dot(activated.T, cotangent, preferred_element_type=jnp.float32).reshape(
        owners, ff_share, model_width
    )
    col_sums = lax.psum_scatter(
        jnp.concatenate([out_term, down_term], axis=1).reshape(owners * share_rows, model_width),
        ("seq", "fsdp"),
        scatter_dimension=0,
        tiled=True,
    )
    out_final = col_sums[:query_share]
    down_final = col_sums[query_share:]
    vectors = (
        lax.psum_scatter(gain_one_grad, ("seq", "fsdp"), scatter_dimension=0, tiled=True),
        lax.psum_scatter(query_b_grad, ("seq", "fsdp"), scatter_dimension=0, tiled=True),
        lax.psum_scatter(key_b_grad, ("seq", "fsdp"), scatter_dimension=0, tiled=True),
        lax.psum_scatter(value_b_grad, ("seq", "fsdp"), scatter_dimension=0, tiled=True),
        lax.psum_scatter(gain_two_grad, ("seq", "fsdp"), scatter_dimension=0, tiled=True),
    )
    return (
        layer_out,
        input_grad,
        vectors[0],
        query_w_grad,
        vectors[1],
        key_w_grad,
        vectors[2],
        value_w_grad,
        vectors[3],
        out_final,
        vectors[4],
        gate_final,
        up_final,
        down_final,
    )


def solution(mesh):
    in_specs = (
        P(("seq", "fsdp"), None),
        P(("seq", "fsdp"), None),
        P(),
        P(("seq", "fsdp")),
        P(("seq", "fsdp"), None),
        P(("seq", "fsdp")),
        P(("seq", "fsdp"), None),
        P(("seq", "fsdp")),
        P(("seq", "fsdp"), None),
        P(("seq", "fsdp")),
        P(("seq", "fsdp"), None),
        P(("seq", "fsdp")),
        P(("seq", "fsdp"), None),
        P(("seq", "fsdp"), None),
        P(("seq", "fsdp"), None),
    )
    out_specs = (
        P(("seq", "fsdp"), None),
        P(("seq", "fsdp"), None),
        P(("seq", "fsdp")),
        P(("seq", "fsdp"), None),
        P(("seq", "fsdp")),
        P(("seq", "fsdp"), None),
        P(("seq", "fsdp")),
        P(("seq", "fsdp"), None),
        P(("seq", "fsdp")),
        P(("seq", "fsdp"), None),
        P(("seq", "fsdp")),
        P(("seq", "fsdp"), None),
        P(("seq", "fsdp"), None),
        P(("seq", "fsdp"), None),
    )
    return jax.shard_map(shards, mesh=mesh, in_specs=in_specs, out_specs=out_specs, check_vma=False)
```

profile of v0, /device:TPU:0, one launch (start us, length us, event | category | flops | bytes accessed | tf_op | source)
XLA Modules:
  0.0 3172.0 jit_solution(339632060756462493)
XLA Ops:
  12.7 42.2 %all-reduce.12 = (bf16[256]{0:T(256)(128)(2,1)S(1)}, bf16[1536]{0:T(1024)(128)(2,1)S(1)}, bf16[256]{0:T(256)(128)(2,1)S(1)}, bf16[1536]{0:T(1024)(128)(2,1)S(1)}, bf16[1536]{0:T(1024)(128)(2,1)S(1)}) all-reduce(bf16[256]{0:T(256)(128)(2,1)S(1)} %dynamic-update-slice.1, ...), channel_id=1, replica_groups=mesh['seq'=8,'fsdp'=4] {'seq','fsdp'}, use_global_device_ids=true, to_apply=%add.1 | all-reduce | flops 5120 | bytes 20480
  54.9 42.7 %all_gather.52 = bf16[1536,256]{1,0:T(8,128)(2,1)S(1)} all-gather(bf16[48,256]{1,0:T(8,128)(2,1)} %param.39), channel_id=1, replica_groups=mesh['seq'=8,'fsdp'=4] {'seq','fsdp'}, dimensions={0}, use_global_device_ids=true | all-gather | bytes 811008 | tf_op jit(solution)/shard_map/all_gather | solution.py:93
  103.9 39.5 %all_gather.55 = bf16[1536,256]{1,0:T(8,128)(2,1)S(1)} all-gather(bf16[48,256]{1,0:T(8,128)(2,1)} %param.37), channel_id=1, replica_groups=mesh['seq'=8,'fsdp'=4] {'seq','fsdp'}, dimensions={0}, use_global_device_ids=true | all-gather | bytes 811008 | tf_op jit(solution)/shard_map/all_gather | solution.py:91
  156.9 62.3 %all-gather.12.cloned.1.call-done = bf16[1536,1536]{1,0:T(8,128)(2,1)} async-done(((bf16[48,1536]{1,0:T(8,128)(2,1)}), bf16[1536,1536]{1,0:T(8,128)(2,1)}) %all-gather.12.cloned.1.call-update) | async-done | bytes 4718608 | tf_op jit(solution)/shard_map/all_gather | solution.py:89
  225.0 49.6 %all-gather.10.cloned.1.call-done = bf16[4096,256]{0,1:T(8,128)(2,1)} async-done(((bf16[128,256]{0,1:T(8,128)(2,1)}), bf16[4096,256]{0,1:T(8,128)(2,1)}) %all-gather.10.cloned.1.call-update) | async-done | bytes 2097168 | tf_op jit(solution)/shard_map/all_gather | solution.py:121
  290.5 49.5 %all-gather.14.cloned.1.call-done = bf16[1536,1536]{1,0:T(8,128)(2,1)} async-done(((bf16[48,1536]{1,0:T(8,128)(2,1)}), bf16[1536,1536]{1,0:T(8,128)(2,1)}) %all-gather.14.cloned.1.call-update) | async-done | bytes 4718608 | tf_op jit(solution)/shard_map/all_gather | solution.py:95
  344.4 163.2 %all-gather.18.cloned.1.call-done = bf16[1536,8960]{1,0:T(8,128)(2,1)} async-done(((bf16[48,8960]{1,0:T(8,128)(2,1)}), bf16[1536,8960]{1,0:T(8,128)(2,1)}) %all-gather.18.cloned.1.call-update) | async-done | bytes 27525136 | tf_op jit(solution)/shard_map/all_gather | solution.py:205
  507.5 14.8 fusion.76
  522.3 152.2 %all-gather.16.cloned.1.call-done = bf16[1536,8960]{1,0:T(8,128)(2,1)} async-done(((bf16[48,8960]{1,0:T(8,128)(2,1)}), bf16[1536,8960]{1,0:T(8,128)(2,1)}) %all-gather.16.cloned.1.call-update) | async-done | bytes 27525136 | tf_op jit(solution)/shard_map/all_gather | solution.py:204
  674.5 14.9 fusion.75
  689.4 152.2 %all-gather.20.cloned.1.call-done = bf16[8960,1536]{1,0:T(8,128)(2,1)} async-done(((bf16[280,1536]{1,0:T(8,128)(2,1)}), bf16[8960,1536]{1,0:T(8,128)(2,1)}) %all-gather.20.cloned.1.call-update) | async-done | bytes 27525136 | tf_op jit(solution)/shard_map/all_gather | solution.py:206
  841.5 18.5 multiply_convert_fusion
  860.0 14.9 fusion.77
  875.0 16.0 multiply_reduce_fusion
  928.0 22.1 fusion.79
  950.1 43.5 %pad_maximum_fusion = f32[32,328,1536]{2,1,0:T(8,128)} fusion(f32[32,280,1536]{2,1,0:T(8,128)} %bitcast.197, f32[32,48,1536]{2,1,0:T(8,128)} %fusion.53), kind=kLoop, calls=%fused_computation.66 | loop fusion | flops 16121856 | bytes 128974848 | tf_op jit(solution)/shard_map/concatenate | solution.py:358
  1001.5 102.8 %reduce-scatter.4.cloned.1.call-done = f32[128,256]{0,1:T(8,128)} async-done(((f32[4096,256]{0,1:T(8,128)}), f32[128,256]{0,1:T(8,128)}) %reduce-scatter.4.cloned.1.call-update) | async-done | bytes 131088 | tf_op jit(solution)/shard_map/reduce_scatter | solution.py:298
  1109.7 133.8 %reduce-scatter.6.cloned.1.call-done = f32[128,256]{0,1:T(8,128)} async-done(((f32[4096,256]{0,1:T(8,128)}), f32[128,256]{0,1:T(8,128)}) %reduce-scatter.6.cloned.1.call-update) | async-done | bytes 131088 | tf_op jit(solution)/shard_map/reduce_scatter | solution.py:299
  1246.1 23.6 convolution_dynamic-update-slice_fusion.1
  1269.7 24.0 convolution_dynamic-update-slice_fusion
  1298.6 12.6 fusion.40
  1312.3 38.8 %all-reduce.11 = (f32[1536]{0:T(1024)S(1)}, f32[1536]{0:T(1024)S(1)}, f32[256]{0:T(256)S(1)}, f32[256]{0:T(256)S(1)}, f32[1536]{0:T(1024)S(1)}) all-reduce(f32[1536]{0:T(1024)S(1)} %get-tuple-element.2086, f32[1536]{0:T(1024)S(1)} %bitcast.223, f32[256]{0:T(256)S(1)} %bitcast.228, ...), channel_id=4, replica_groups=mesh['seq'=8,'fsdp'=4] {'seq','fsdp'}, use_global_device_ids=true, to_apply=%region_37.38.clone | all-reduce | flops 5120 | bytes 40960
  1355.2 826.4 %all-reduce.15.cloned.1.call-done = f32[10496,1536]{1,0:T(8,128)} async-done(((f32[10496,1536]{1,0:T(8,128)}), f32[10496,1536]{1,0:T(8,128)}) %all-reduce.15.cloned.1.call-update) | async-done | bytes 64487440
  2186.2 971.8 %reduce-scatter.8.cloned.1.call-done = f32[48,19968]{1,0:T(8,128)} async-done(((f32[1536,19968]{1,0:T(8,128)}), f32[48,19968]{1,0:T(8,128)}) %reduce-scatter.8.cloned.1.call-update) | async-done | bytes 3833872 | tf_op jit(solution)/shard_map/reduce_scatter | solution.py:326
  (272 shorter events, 176.9 us)
Async XLA Ops:
  7.2 146.8 %all-gather.8.cloned.1.call-start = ((), (), s32[]{:S(2)}) async-start(), calls=%async_computation.3 | async-start | bytes 2162688 | tf_op jit(solution)/shard_map/all_gather | solution.py:122
  8.4 210.8 %copy-start.36 = (f32[128]{0:T(128)}, f32[128]{0:T(128)S(1)}, u32[]{:S(2)}) copy-start(f32[128]{0:T(128)S(1)} %add_rsqrt_fusion.1) | copy-start | bytes 1540
  54.9 164.3 %copy-start.29 = (f32[1536]{0:T(1024)}, f32[1536]{0:T(1024)S(1)}, u32[]{:S(2)}) copy-start(f32[1536]{0:T(1024)S(1)} %convert_element_type.160) | copy-start | bytes 18436
  100.5 118.7 %all-gather.12.cloned.1.call-start = ((), (), s32[]{:S(2)}) async-start(), calls=%async_computation.5 | async-start | bytes 4866048 | tf_op jit(solution)/shard_map/all_gather | solution.py:89
  101.2 173.4 %all-gather.10.cloned.1.call-start = ((), (), s32[]{:S(2)}) async-start(), calls=%async_computation.4 | async-start | bytes 2162688 | tf_op jit(solution)/shard_map/all_gather | solution.py:121
  103.7 119.8 %copy-start.31 = (f32[128,64]{0,1:T(8,128)}, f32[128,64]{0,1:T(8,128)S(1)}, u32[]{:S(2)}) copy-start(f32[128,64]{0,1:T(8,128)S(1)} %get-tuple-element.2227) | copy-start | bytes 98308
  103.8 53.0 %copy-start.27 = (f32[128,64]{1,0:T(8,128)}, f32[128,64]{1,0:T(8,128)S(1)}, u32[]{:S(2)}) copy-start(f32[128,64]{1,0:T(8,128)S(1)} %copy.151) | copy-start | bytes 98308
  144.4 74.9 %copy-start.5 = (bf16[128,1536]{1,0:T(8,128)(2,1)S(1)}, bf16[128,1536]{1,0:T(8,128)(2,1)}, u32[]{:S(2)}) copy-start(bf16[128,1536]{1,0:T(8,128)(2,1)} %param.31) | copy-start | bytes 1179652
  147.1 192.9 %all-gather.14.cloned.1.call-start = ((), (), s32[]{:S(2)}) async-start(), calls=%async_computation.6 | async-start | bytes 4866048 | tf_op jit(solution)/shard_map/all_gather | solution.py:95
  147.7 359.9 %all-gather.18.cloned.1.call-start = ((), (), s32[]{:S(2)}) async-start(), calls=%async_computation.8 | async-start | bytes 28385280 | tf_op jit(solution)/shard_map/all_gather | solution.py:205
  148.2 526.2 %all-gather.16.cloned.1.call-start = ((), (), s32[]{:S(2)}) async-start(), calls=%async_computation.7 | async-start | bytes 28385280 | tf_op jit(solution)/shard_map/all_gather | solution.py:204
  148.8 692.7 %all-gather.20.cloned.1.call-start = ((), (), s32[]{:S(2)}) async-start(), calls=%async_computation.9 | async-start | bytes 28385280 | tf_op jit(solution)/shard_map/all_gather | solution.py:206
  149.6 954.8 %reduce-scatter.4.cloned.1.call-start = ((), (), s32[]{:S(2)}) async-start(), calls=%async_computation.10 | async-start | bytes 4325376 | tf_op jit(solution)/shard_map/reduce_scatter | solution.py:298
  156.9 117.8 %copy-start.41 = (s32[7]{0:T(128)S(1)}, s32[7]{0:T(128)}, u32[]{:S(2)}) copy-start(s32[7]{0:T(128)} %param.33) | copy-start | bytes 88
  288.0 234.3 %copy-start.1 = (bf16[4096,256]{0,1:T(8,128)(2,1)}, bf16[4096,256]{0,1:T(8,128)(2,1)S(1)}, u32[]{:S(2)}) copy-start(bf16[4096,256]{0,1:T(8,128)(2,1)S(1)} %get-tuple-element.2749) | copy-start | bytes 6291460
  344.4 330.1 %copy-start.16 = (bf16[128,1536]{1,0:T(8,128)(2,1)}, bf16[128,1536]{1,0:T(8,128)(2,1)S(1)}, u32[]{:S(2)}) copy-start(bf16[128,1536]{1,0:T(8,128)(2,1)S(1)} %multiply_convert_fusion.3) | copy-start | bytes 1179652
  674.5 167.1 %copy-start.24 = (bf16[128,1536]{1,0:T(8,128)(2,1)S(1)}, bf16[128,1536]{1,0:T(8,128)(2,1)}, u32[]{:S(2)}) copy-start(bf16[128,1536]{1,0:T(8,128)(2,1)} %param.32) | copy-start | bytes 1179652
  921.9 321.6 %reduce-scatter.6.cloned.1.call-start = ((), (), s32[]{:S(2)}) async-start(), calls=%async_computation.11 | async-start | bytes 4325376 | tf_op jit(solution)/shard_map/reduce_scatter | solution.py:299
  922.6 1259.0 %all-reduce.15.cloned.1.call-start = ((), (), s32[]{:S(2)}) async-start(), calls=%async_computation.13 | async-start | bytes 128974848
  993.7 2164.3 %reduce-scatter.8.cloned.1.call-start = ((), (), s32[]{:S(2)}) async-start(), calls=%async_computation.12 | async-start | bytes 126517248 | tf_op jit(solution)/shard_map/reduce_scatter | solution.py:326
  996.3 109.3 %copy-start.28 = (f32[128,64]{1,0:T(8,128)S(1)}, f32[128,64]{1,0:T(8,128)}, u32[]{:S(2)}) copy-start(f32[128,64]{1,0:T(8,128)} %copy-done.27) | copy-start | bytes 98308
  1001.5 244.6 %copy-start.10 = (bf16[128,8960]{1,0:T(8,128)(2,1)S(1)}, bf16[128,8960]{1,0:T(8,128)(2,1)}, u32[]{:S(2)}) copy-start(bf16[128,8960]{1,0:T(8,128)(2,1)} %get-tuple-element.2209) | copy-start | bytes 6881284
  1001.5 244.6 %copy-start.17 = (bf16[128,1536]{1,0:T(8,128)(2,1)S(1)}, bf16[128,1536]{1,0:T(8,128)(2,1)}, u32[]{:S(2)}) copy-start(bf16[128,1536]{1,0:T(8,128)(2,1)} %copy-done.16) | copy-start | bytes 1179652
  1311.2 42.9 %copy-start.15 = (f32[128,1536]{1,0:T(8,128)S(1)}, f32[128,1536]{1,0:T(8,128)}, u32[]{:S(2)}) copy-start(f32[128,1536]{1,0:T(8,128)} %copy-done.13) | copy-start | bytes 2359300
  (29 other events, 177.2 us)
Sparse Core Ops, SparseCore 0:
  100.6 53.2 all-gather.7
  156.8 62.3 all-gather.11
  222.6 52.0 all-gather.9
  277.4 62.4 all-gather.13
  342.8 164.7 all-gather.17
  510.3 164.1 all-gather.15
  677.4 164.1 all-gather.19
  922.0 182.3 reduce-scatter.3
  1106.6 136.8 reduce-scatter.5
  1249.8 931.8 all-reduce.14
  2188.1 969.8 reduce-scatter.7
where the time goes:
time: 3180 us; the launch traced here: 3170 us
  waiting for transfers between devices  2670 us (84%)
  matrix products  211 us (7%)
  blocking collectives  163 us (5%)
  other arithmetic  61.6 us (2%)
  local copies, waits for them, and re-layouts  46.5 us (1%)
    reduce_scatter x1, waiting for transfers between devices, shards(): lax.psum_scatter(jnp.concatenate([jnp.dot(first_part, grad_query, preferr...  972 us
    unnamed x12, waiting for transfers between devices  830 us
    all_gather x1, waiting for transfers between devices, shards(): lax.all_gather(up_weight, ('seq', 'fsdp'), axis=0, tiled=True)  163 us
    all_gather x1, waiting for transfers between devices, shards(): lax.all_gather(gate_weight, ('seq', 'fsdp'), axis=0, tiled=True)  152 us
    all_gather x1, waiting for transfers between devices, shards(): lax.all_gather(down_weight, ('seq', 'fsdp'), axis=0, tiled=True)  152 us
    reduce_scatter x1, waiting for transfers between devices, shards(): lax.psum_scatter(value_part, ('seq', 'fsdp'), scatter_dimension=0, tiled=...  134 us
    reduce_scatter x1, waiting for transfers between devices, shards(): lax.psum_scatter(key_part, ('seq', 'fsdp'), scatter_dimension=0, tiled=True)  103 us
    unnamed x2, blocking collectives  81.1 us
  transfers between devices with their start and end apart: 11, of which 11 were waited for; matrix products, arithmetic and copies ran while one was open for 7% of the time, Pallas kernels for 0%

commit v1 on v0

v1 whole, which is shorter than its diff:
```python
import functools

import jax
import jax.numpy as jnp
from jax import lax
from jax.experimental import pallas as pl
from jax.experimental.pallas import tpu as pltpu
from jax.sharding import PartitionSpec as P

HEADS = 12
KV_HEADS = 2
HEAD_DIM = 128
GROUP = HEADS // KV_HEADS
EPSILON = 1e-06
ROPE_BASE = 10000.0
LOG2E = 1.4426950408889634
AXES = ("seq", "fsdp")
VMEM_LIMIT = 56 << 20
F32 = jnp.float32
BF16 = jnp.bfloat16
DMA = pltpu.SemaphoreType.DMA


class Place:
    def __init__(self, depth):
        self.depth = depth
        self.s = lax.axis_index("seq")
        self.f = lax.axis_index("fsdp")
        self.z = lax.div(self.s, 2)
        self.x = lax.rem(self.s, 2)
        self.y = lax.div(self.f, 2)
        self.c = lax.rem(self.f, 2)
        self.up = self.z + 1 < depth
        self.down = self.z > 0

    def flip_x(self):
        return (self.s + 1 - 2 * self.x, self.f)

    def flip_y(self):
        return (self.s, self.f + 2 - 4 * self.y)

    def flip_c(self):
        return (self.s, self.f + 1 - 2 * self.c)

    def z_up(self):
        return (self.s + 2, self.f)

    def z_down(self):
        return (self.s - 2, self.f)

    def first(self):
        return (
            self.s + (1 - self.c) * (1 - 2 * self.x),
            self.f + self.c * (2 - 4 * self.y),
        )

    def second(self):
        return (
            self.s + self.c * (1 - 2 * self.x),
            self.f + (1 - self.c) * (2 - 4 * self.y),
        )

    def corner(self, i, j):
        over_x = i * (1 - self.c) + j * self.c
        over_y = j * (1 - self.c) + i * self.c
        return (self.x + over_x * (1 - 2 * self.x), self.y + over_y * (1 - 2 * self.y))

    def wave(self, k):
        if k == 0:
            return [(self.z, None)]
        return [(self.z - k, self.z - k >= 0), (self.z + k, self.z + k < self.depth)]


def guard(condition, body):
    if condition is None:
        body()
    else:
        pl.when(condition)(body)


def greet(place, others=()):
    barrier = pltpu.get_barrier_semaphore()
    partners = [place.flip_x(), place.flip_y(), place.flip_c(), *others]
    for partner in partners:
        pl.semaphore_signal(barrier, inc=1, device_id=partner, device_id_type=pl.DeviceIdType.MESH)

    def tell_up():
        pl.semaphore_signal(
            barrier, inc=1, device_id=place.z_up(), device_id_type=pl.DeviceIdType.MESH
        )

    def tell_down():
        pl.semaphore_signal(
            barrier, inc=1, device_id=place.z_down(), device_id_type=pl.DeviceIdType.MESH
        )

    pl.when(place.up)(tell_up)
    pl.when(place.down)(tell_down)
    pl.semaphore_wait(
        barrier, len(partners) + place.up.astype(jnp.int32) + place.down.astype(jnp.int32)
    )


def remote(src, dst, send_sem, recv_sem, device):
    return pltpu.make_async_remote_copy(
        src_ref=src,
        dst_ref=dst,
        send_sem=send_sem,
        recv_sem=recv_sem,
        device_id=device,
        device_id_type=pl.DeviceIdType.MESH,
    )


def add_into(target, term, rows):
    step = 16 if rows % 16 == 0 else rows

    def body(number, carry):
        at = pl.ds(pl.multiple_of(number * step, step), step)
        target[at, :] = (target[at, :].astype(F32) + term[at, :].astype(F32)).astype(BF16)
        return carry

    lax.fori_loop(0, rows // step, body, 0)


class Gather:
    def __init__(self, place, wide, own, out, sems):
        self.place, self.wide, self.own, self.out, self.sems = place, wide, own, out, sems
        self.sent = []

    @staticmethod
    def semaphores(depth, wide):
        base = [DMA((1,)), DMA((2 * depth,)), DMA((depth,)), DMA((depth,)), DMA((depth,))]
        if wide:
            base += [DMA((2 * depth,)), DMA((2 * depth,)), DMA((4 * depth,)), DMA((4 * depth,))]
        return base

    def at(self, zi, i, j):
        place = self.place
        if self.wide:
            x, y = place.corner(i, j)
            return self.out.at[zi, x, y, place.c]
        return self.out.at[zi, place.x + i * (1 - 2 * place.x)]

    def send(self, src, dst, send_sem, recv_sem, device, condition):
        copy = remote(src, dst, send_sem, recv_sem, device)
        guard(condition, copy.start)
        self.sent.append((copy, condition))

    def local(self):
        copy = pltpu.make_async_copy(
            self.own, self.at(self.place.z, 0, 0), self.sems[0].at[0]
        )
        return copy

    def arrive(self, k):
        place, depth = self.place, self.place.depth
        z_send, z_recv, a_send, a_recv = self.sems[1:5]
        across = place.first() if self.wide else place.flip_x()
        for side, (zi, ok) in enumerate(place.wave(k)):
            block = self.at(zi, 0, 0)
            source = self.own if k == 0 else block
            if k > 0:
                landed = remote(block, block, z_send.at[0], z_recv.at[zi], place.z_up())
                guard(ok, landed.wait_recv)
            both = lambda a, b: a if b is None else jnp.logical_and(a, b)
            if k == 0 or side == 0:
                self.send(
                    source, block, z_send.at[k], z_recv.at[zi], place.z_up(), both(place.up, ok)
                )
            if k == 0 or side == 1:
                self.send(
                    source,
                    block,
                    z_send.at[depth + k],
                    z_recv.at[zi],
                    place.z_down(),
                    both(place.down, ok),
                )
            self.send(source, block, a_send.at[zi], a_recv.at[zi], across, ok)
            if self.wide:
                b_send, b_recv = self.sems[5:7]
                self.send(
                    source, block, b_send.at[2 * zi], b_recv.at[2 * zi], place.second(), ok
                )

    def across(self, k):
        place = self.place
        a_send, a_recv = self.sems[3:5]
        for zi, ok in place.wave(k):
            block = self.at(zi, 1, 0)
            landed = remote(block, block, a_send.at[0], a_recv.at[zi], place.first())
            guard(ok, landed.wait_recv)
            if self.wide:
                b_send, b_recv = self.sems[5:7]
                self.send(
                    block, block, b_send.at[2 * zi + 1], b_recv.at[2 * zi + 1], place.second(), ok
                )

    def hand(self, k):
        place = self.place
        b_send, b_recv, c_send, c_recv = self.sems[5:9]
        for zi, ok in place.wave(k):
            for i in range(2):
                block = self.at(zi, i, 1)
                landed = remote(block, block, b_send.at[0], b_recv.at[2 * zi + i], place.second())
                guard(ok, landed.wait_recv)
            for x in range(2):
                for y in range(2):
                    block = self.out.at[zi, x, y, place.c]
                    slot = 4 * zi + 2 * x + y
                    self.send(
                        block, block, c_send.at[slot], c_recv.at[slot], place.flip_c(), ok
                    )

    def take(self, k):
        place = self.place
        c_send, c_recv = self.sems[7:9]
        for zi, ok in place.wave(k):
            for x in range(2):
                for y in range(2):
                    block = self.out.at[zi, x, y, 1 - place.c]
                    slot = 4 * zi + 2 * x + y
                    landed = remote(block, block, c_send.at[0], c_recv.at[slot], place.flip_c())
                    guard(ok, landed.wait_recv)

    def settle(self):
        for copy, condition in self.sent:
            guard(condition, copy.wait_send)


def drive_gathers(place, gathers):
    depth = place.depth
    locals_ = [gather.local() for gather in gathers]
    for copy in locals_:
        copy.start()
    for step in range(depth + 3):
        for gather in gathers:
            if step < depth:
                gather.arrive(step)
        if step == 0:
            for copy in locals_:
                copy.wait()
        for gather in gathers:
            if 0 <= step - 1 < depth:
                gather.across(step - 1)
        for gather in gathers:
            if gather.wide and 0 <= step - 2 < depth:
                gather.hand(step - 2)
        for gather in gathers:
            if gather.wide and 0 <= step - 3 < depth:
                gather.take(step - 3)
    for gather in gathers:
        gather.settle()


def gather_shape(depth, wide, own):
    lead = (depth, 2, 2, 2) if wide else (depth, 2)
    return jax.ShapeDtypeStruct(lead + own.shape, own.dtype)


def call_gathers(depth, collective_id, wides, owns):
    def kernel(*refs):
        count = len(owns)
        place = Place(depth)
        greet(place)
        gathers, used = [], 2 * count
        for number, wide in enumerate(wides):
            need = len(Gather.semaphores(depth, wide))
            gathers.append(
                Gather(place, wide, refs[number], refs[count + number], refs[used : used + need])
            )
            used += need
        drive_gathers(place, gathers)

    scratch = []
    for wide in wides:
        scratch += Gather.semaphores(depth, wide)
    return pl.pallas_call(
        kernel,
        out_shape=[gather_shape(depth, wide, own) for wide, own in zip(wides, owns)],
        in_specs=[pl.BlockSpec(memory_space=pl.ANY)] * len(owns),
        out_specs=[pl.BlockSpec(memory_space=pl.ANY)] * len(owns),
        scratch_shapes=scratch,
        compiler_params=pltpu.CompilerParams(
            collective_id=collective_id, has_side_effects=True, vmem_limit_bytes=VMEM_LIMIT
        ),
    )(*owns)


def start_kernel(depth, *refs):
    (pack, cot, wide_in, down_in, pack_out, cot_out, wide_out, down_out), sems = refs[:8], refs[8:]
    place = Place(depth)
    count = 2 * depth
    partners = []
    for offset in range(1, count):
        partners.append((lax.rem(place.s + offset, count), place.f))
    greet(place, partners)
    first = len(Gather.semaphores(depth, True))
    second = first + len(Gather.semaphores(depth, False))
    gathers = [
        Gather(place, True, pack, pack_out, sems[:first]),
        Gather(place, False, cot, cot_out, sems[first:second]),
    ]
    local_sem, e_send, e_recv, y_send, y_recv, c_send, c_recv, d_sem, d_send, d_recv = sems[second:]
    sent = []

    def send(src, dst, send_sem, recv_sem, device):
        copy = remote(src, dst, send_sem, recv_sem, device)
        copy.start()
        sent.append(copy)

    locals_ = [gather.local() for gather in gathers]
    locals_.append(
        pltpu.make_async_copy(
            wide_in.at[:, place.s], wide_out.at[:, place.s, place.f], local_sem.at[0]
        )
    )
    locals_.append(pltpu.make_async_copy(down_in, down_out.at[place.f], d_sem.at[0]))
    for copy in locals_:
        copy.start()

    y_f = place.f + 2 - 4 * place.y
    c_f = place.f + 1 - 2 * place.c
    yc_f = y_f + 1 - 2 * place.c

    def exchange(offset):
        to = lax.rem(place.s + offset, count)
        send(
            wide_in.at[:, to],
            wide_out.at[:, place.s, place.f],
            e_send.at[offset],
            e_recv.at[offset],
            (to, place.f),
        )

    def onward(offset):
        origin = lax.rem(place.s + count - offset, count)
        block = wide_out.at[:, origin, place.f]
        if offset > 0:
            remote(block, block, e_send.at[0], e_recv.at[offset], place.flip_y()).wait_recv()
        send(block, block, y_send.at[offset], y_recv.at[offset], place.flip_y())
        send(block, block, c_send.at[2 * offset], c_recv.at[2 * offset], place.flip_c())

    def sideways(offset):
        origin = lax.rem(place.s + count - offset, count)
        block = wide_out.at[:, origin, y_f]
        remote(block, block, y_send.at[0], y_recv.at[offset], place.flip_y()).wait_recv()
        send(block, block, c_send.at[2 * offset + 1], c_recv.at[2 * offset + 1], place.flip_c())

    def last(offset):
        origin = lax.rem(place.s + count - offset, count)
        for slot, owner in ((2 * offset, c_f), (2 * offset + 1, yc_f)):
            block = wide_out.at[:, origin, owner]
            remote(block, block, c_send.at[0], c_recv.at[slot], place.flip_c()).wait_recv()

    for gather in gathers:
        gather.arrive(0)
    send(down_in, down_out.at[place.f], d_send.at[0], d_recv.at[0], place.flip_y())
    send(down_in, down_out.at[place.f], d_send.at[1], d_recv.at[1], place.flip_c())
    for offset in range(1, count):
        exchange(offset)
    for copy in locals_:
        copy.wait()
    onward(0)
    total = depth + 3
    for step in range(1, total):
        for gather in gathers:
            if step < depth:
                gather.arrive(step)
        for gather in gathers:
            if 0 <= step - 1 < depth:
                gather.across(step - 1)
        for gather in gathers:
            if gather.wide and 0 <= step - 2 < depth:
                gather.hand(step - 2)
        for gather in gathers:
            if gather.wide and 0 <= step - 3 < depth:
                gather.take(step - 3)
    block = down_out.at[y_f]
    remote(block, block, d_send.at[0], d_recv.at[0], place.flip_y()).wait_recv()
    send(block, block, d_send.at[2], d_recv.at[2], place.flip_c())
    for offset in range(1, count):
        onward(offset)
        sideways(offset - 1)
    sideways(count - 1)
    for offset in range(count):
        last(offset)
    for slot, owner in ((1, c_f), (2, yc_f)):
        block = down_out.at[owner]
        remote(block, block, d_send.at[0], d_recv.at[slot], place.flip_c()).wait_recv()
    for gather in gathers:
        gather.settle()
    for copy in sent:
        copy.wait_send()


def call_start(depth, collective_id, pack, cot, wide, down):
    count = 2 * depth
    _, _, rows, columns = wide.shape
    scratch = Gather.semaphores(depth, True) + Gather.semaphores(depth, False)
    scratch += [DMA((1,)), DMA((count,)), DMA((count,)), DMA((count,)), DMA((count,))]
    scratch += [DMA((2 * count,)), DMA((2 * count,)), DMA((1,)), DMA((3,)), DMA((3,))]
    return pl.pallas_call(
        functools.partial(start_kernel, depth),
        out_shape=[
            gather_shape(depth, True, pack),
            gather_shape(depth, False, cot),
            jax.ShapeDtypeStruct((2, count, 4, rows, columns), BF16),
            jax.ShapeDtypeStruct((4,) + down.shape, BF16),
        ],
        in_specs=[pl.BlockSpec(memory_space=pl.ANY)] * 4,
        out_specs=[pl.BlockSpec(memory_space=pl.ANY)] * 4,
        scratch_shapes=scratch,
        compiler_params=pltpu.CompilerParams(
            collective_id=collective_id, has_side_effects=True, vmem_limit_bytes=VMEM_LIMIT
        ),
    )(pack, cot, wide, down)


class Reduce:
    def __init__(self, place, wide, rows, own, out, buffers, sems):
        self.place, self.wide, self.rows = place, wide, rows
        self.own, self.out, self.buffers, self.sems = own, out, buffers, sems
        self.sent = []

    @staticmethod
    def scratch(depth, wide, block):
        buffers = [
            pltpu.VMEM((depth,) + block, BF16),
            pltpu.VMEM((depth + 1,) + block, BF16),
        ]
        sems = [DMA((depth,)), DMA((depth,)), DMA((2 * depth,)), DMA((2 * depth,))]
        if wide:
            buffers += [
                pltpu.VMEM((depth, 2, 2) + block, BF16),
                pltpu.VMEM((depth, 2) + block, BF16),
            ]
            sems += [DMA((4 * depth,)), DMA((4 * depth,)), DMA((2 * depth,)), DMA((2 * depth,))]
        return buffers, sems

    def send(self, src, dst, send_sem, recv_sem, device, condition):
        copy = remote(src, dst, send_sem, recv_sem, device)
        guard(condition, copy.start)
        self.sent.append((copy, condition))

    def cores(self, k):
        place = self.place
        c_send, c_recv = self.sems[4:6]
        got = self.buffers[2]
        for zi, ok in place.wave(k):
            for x in range(2):
                for y in range(2):
                    slot = 4 * zi + 2 * x + y
                    self.send(
                        self.own.at[zi, x, y, 1 - place.c],
                        got.at[zi, x, y],
                        c_send.at[slot],
                        c_recv.at[slot],
                        place.flip_c(),
                        ok,
                    )

    def over_second(self, k):
        place = self.place
        c_send, c_recv, b_send, b_recv = self.sems[4:8]
        got, next_ = self.buffers[2:4]
        for zi, ok in place.wave(k):

            def body(zi=zi):
                for j in (1, 0):
                    for i in (1, 0):
                        x, y = place.corner(i, j)
                        block = got.at[zi, x, y]
                        slot = 4 * zi + 2 * x + y
                        remote(
                            block, block, c_send.at[0], c_recv.at[slot], place.flip_c()
                        ).wait_recv()
                        add_into(block, self.own.at[zi, x, y, place.c], self.rows)
                        if j == 1:
                            remote(
                                block,
                                next_.at[zi, i],
                                b_send.at[2 * zi + i],
                                b_recv.at[2 * zi + i],
                                place.second(),
                            ).start()

            guard(ok, body)
            for i in (1, 0):
                x, y = place.corner(i, 1)
                copy = remote(
                    got.at[zi, x, y],
                    next_.at[zi, i],
                    b_send.at[2 * zi + i],
                    b_recv.at[2 * zi + i],
                    place.second(),
                )
                self.sent.append((copy, ok))

    def over_first(self, k):
        place = self.place
        a_send, a_recv = self.sems[0:2]
        got = self.buffers[0]
        for zi, ok in place.wave(k):
            if self.wide:
                b_send, b_recv = self.sems[6:8]
                before, held = self.buffers[2:4]

                def body(zi=zi):
                    for i in (1, 0):
                        block = held.at[zi, i]
                        x, y = place.corner(i, 0)
                        remote(
                            block, block, b_send.at[0], b_recv.at[2 * zi + i], place.second()
                        ).wait_recv()
                        add_into(block, before.at[zi, x, y], self.rows)
                        if i == 1:
                            remote(
                                block, got.at[zi], a_send.at[zi], a_recv.at[zi], place.first()
                            ).start()

                guard(ok, body)
                copy = remote(
                    held.at[zi, 1], got.at[zi], a_send.at[zi], a_recv.at[zi], place.first()
                )
                self.sent.append((copy, ok))
            else:
                self.send(
                    self.own.at[zi, 1 - place.x],
                    got.at[zi],
                    a_send.at[zi],
                    a_recv.at[zi],
                    place.flip_x(),
                    ok,
                )

    def along(self, k):
        place, depth = self.place, self.place.depth
        a_send, a_recv, z_send, z_recv = self.sems[0:4]
        held, line = self.buffers[0:2]
        for side, (zi, ok) in enumerate(place.wave(k)):
            block = held.at[zi]

            def body(zi=zi, side=side, block=block):
                remote(block, block, a_send.at[0], a_recv.at[zi], place.first()).wait_recv()
                if self.wide:
                    add_into(block, self.buffers[3].at[zi, 0], self.rows)
                else:
                    add_into(block, self.own.at[zi, place.x], self.rows)

                def more(direction):
                    slot = direction * depth + zi
                    term = line.at[depth if k == 0 and direction == 1 else zi]
                    remote(term, term, z_send.at[0], z_recv.at[slot], place.z_up()).wait_recv()
                    add_into(block, term, self.rows)

                def pass_on(direction, to):
                    slot = direction * depth + zi
                    there = line.at[depth if k == 1 and direction == 1 else zi]
                    remote(block, there, z_send.at[slot], z_recv.at[slot], to).start()

                if k == 0:
                    pl.when(place.down)(functools.partial(more, 0))
                    pl.when(place.up)(functools.partial(more, 1))
                elif side == 0:
                    pl.when(place.up)(functools.partial(more, 1))
                    pass_on(1, place.z_down())
                else:
                    pl.when(place.down)(functools.partial(more, 0))
                    pass_on(0, place.z_up())

            guard(ok, body)
            if k > 0:
                direction = 1 - side
                slot = direction * depth + zi
                to = place.z_up() if side == 1 else place.z_down()
                there = line.at[depth if k == 1 and direction == 1 else zi]
                copy = remote(block, there, z_send.at[slot], z_recv.at[slot], to)
                self.sent.append((copy, ok))

    def finish(self):
        self.out[...] = self.buffers[0][self.place.z].astype(self.out.dtype)

    def settle(self):
        for copy, condition in self.sent:
            guard(condition, copy.wait_send)


def drive_reduces(place, reduces):
    depth = place.depth
    order = list(range(depth - 1, -1, -1))
    for reduce in reduces:
        for k in order:
            reduce.cores(k) if reduce.wide else reduce.over_first(k)
    for step in range(depth + 2):
        for reduce in reduces:
            if not reduce.wide:
                if step < depth:
                    reduce.along(order[step])
                continue
            if step < depth:
                reduce.over_second(order[step])
            if 0 <= step - 1 < depth:
                reduce.over_first(order[step - 1])
            if 0 <= step - 2 < depth:
                reduce.along(order[step - 2])
    for reduce in reduces:
        reduce.finish()
    for reduce in reduces:
        reduce.settle()


def call_reduces(depth, collective_id, wides, owns):
    count = len(owns)
    blocks = [own.shape[-2:] for own in owns]
    parts = [Reduce.scratch(depth, wide, block) for wide, block in zip(wides, blocks)]
    scratch = []
    for buffers, sems in parts:
        scratch += buffers + sems

    def kernel(*refs):
        place = Place(depth)
        greet(place)
        reduces, used = [], 2 * count
        for number, (buffers, sems) in enumerate(parts):
            middle, end = used + len(buffers), used + len(buffers) + len(sems)
            reduces.append(
                Reduce(
                    place,
                    wides[number],
                    blocks[number][0],
                    refs[number],
                    refs[count + number],
                    refs[used:middle],
                    refs[middle:end],
                )
            )
            used = end
        drive_reduces(place, reduces)

    return pl.pallas_call(
        kernel,
        out_shape=[jax.ShapeDtypeStruct(block, F32) for block in blocks],
        in_specs=[pl.BlockSpec(memory_space=pltpu.VMEM)] * count,
        out_specs=[pl.BlockSpec(memory_space=pltpu.VMEM)] * count,
        scratch_shapes=scratch,
        compiler_params=pltpu.CompilerParams(
            collective_id=collective_id, has_side_effects=True, vmem_limit_bytes=VMEM_LIMIT
        ),
    )(*owns)


def end_kernel(depth, shapes, *refs):
    pack, wide, down, pack_out, wide_out, down_out = refs[:6]
    block, wide_block, down_block = shapes
    buffers, sems = Reduce.scratch(depth, True, block)
    used = 6 + len(buffers)
    place = Place(depth)
    count = 2 * depth
    partners = []
    for offset in range(1, count):
        partners.append((lax.rem(place.s + offset, count), place.f))
    greet(place, partners)
    reduce = Reduce(
        place, True, block[0], pack, pack_out, refs[6:used], refs[used : used + len(sems)]
    )
    used += len(sems)
    w_core, w_y, d_core, d_y = refs[used : used + 4]
    wc_send, wc_recv, wy_send, wy_recv, e_send, e_recv, e_sem = refs[used + 4 : used + 11]
    dc_send, dc_recv, dy_send, dy_recv = refs[used + 11 :]
    sent = []
    wide_rows, down_rows = wide_block[1], down_block[0]

    def send(src, dst, send_sem, recv_sem, device):
        copy = remote(src, dst, send_sem, recv_sem, device)
        copy.start()
        sent.append(copy)

    def landed(ref, recv_sem):
        remote(ref, ref, e_send.at[0], recv_sem, place.flip_c()).wait_recv()

    mine_y, other_y = place.y, 1 - place.y
    offsets = list(range(1, count)) + [0]
    for y in range(2):
        side = other_y if y == 0 else mine_y
        send(
            down.at[2 * side + 1 - place.c],
            d_core.at[side],
            dc_send.at[side],
            dc_recv.at[side],
            place.flip_c(),
        )
    for offset in offsets:
        to = lax.rem(place.s + offset, count)
        for y in range(2):
            send(
                wide.at[:, to, 2 * y + 1 - place.c],
                w_core.at[y, offset],
                wc_send.at[2 * offset + y],
                wc_recv.at[2 * offset + y],
                place.flip_c(),
            )
    order = list(range(depth - 1, -1, -1))
    for k in order:
        reduce.cores(k)

    def wide_add(target, term):
        for part in range(2):
            add_into(target.at[part], term.at[part], wide_rows)

    def wide_cores(offset):
        to = lax.rem(place.s + offset, count)
        for side in (other_y, mine_y):
            landed(w_core.at[side, offset], wc_recv.at[2 * offset + side])
            wide_add(w_core.at[side, offset], wide.at[:, to, 2 * side + place.c])
            if side is other_y:
                send(
                    w_core.at[side, offset],
                    w_y.at[offset],
                    wy_send.at[offset],
                    wy_recv.at[offset],
                    place.flip_y(),
                )

    def wide_across(offset):
        landed(w_y.at[offset], wy_recv.at[offset])
        wide_add(w_y.at[offset], w_core.at[mine_y, offset])
        to = lax.rem(place.s + offset, count)
        if offset > 0:
            send(
                w_y.at[offset],
                wide_out.at[place.s],
                e_send.at[offset],
                e_recv.at[offset],
                (to, place.f),
            )
        else:
            pltpu.make_async_copy(w_y.at[0], wide_out.at[place.s], e_sem.at[0]).start()

    for offset in offsets[: count // 2]:
        wide_cores(offset)
    for step in range(depth):
        reduce.over_second(order[step])
        if step >= 1:
            reduce.over_first(order[step - 1])
        if step == 0:
            for offset in offsets[count // 2 :]:
                wide_cores(offset)
            for side in (other_y, mine_y):
                landed(d_core.at[side], dc_recv.at[side])
                add_into(d_core.at[side], down.at[2 * side + place.c], down_rows)
                if side is other_y:
                    send(d_core.at[side], d_y.at[0], dy_send.at[0], dy_recv.at[0], place.flip_y())
        for offset in offsets[step * count // depth : (step + 1) * count // depth]:
            wide_across(offset)
        if step >= 2:
            reduce.along(order[step - 2])
    reduce.over_first(order[depth - 1])
    for step in range(max(depth - 2, 0), depth):
        reduce.along(order[step])
    reduce.finish()
    landed(d_y.at[0], dy_recv.at[0])
    down_out[...] = d_y[0].astype(F32) + d_core[mine_y].astype(F32)
    for offset in range(1, count):
        origin = lax.rem(place.s + count - offset, count)
        landed(wide_out.at[origin], e_recv.at[offset])
    pltpu.make_async_copy(w_y.at[0], wide_out.at[place.s], e_sem.at[0]).wait()
    reduce.settle()
    for copy in sent:
        copy.wait_send()


def call_end(depth, collective_id, pack, wide, down):
    count = 2 * depth
    block = pack.shape[-2:]
    wide_block = (2,) + wide.shape[-2:]
    down_block = down.shape[-2:]
    buffers, sems = Reduce.scratch(depth, True, block)
    scratch = buffers + sems
    scratch += [
        pltpu.VMEM((2, count) + wide_block, BF16),
        pltpu.VMEM((count,) + wide_block, BF16),
        pltpu.VMEM((2,) + down_block, BF16),
        pltpu.VMEM((1,) + down_block, BF16),
    ]
    scratch += [DMA((2 * count,)), DMA((2 * count,)), DMA((count,)), DMA((count,))]
    scratch += [DMA((count,)), DMA((count,)), DMA((1,))]
    scratch += [DMA((2,)), DMA((2,)), DMA((1,)), DMA((1,))]
    vmem = pl.BlockSpec(memory_space=pltpu.VMEM)
    return pl.pallas_call(
        functools.partial(end_kernel, depth, (block, wide_block, down_block)),
        out_shape=[
            jax.ShapeDtypeStruct(block, F32),
            jax.ShapeDtypeStruct((count,) + wide_block, BF16),
            jax.ShapeDtypeStruct(down_block, F32),
        ],
        in_specs=[vmem] * 3,
        out_specs=[vmem, vmem, vmem],
        scratch_shapes=scratch,
        compiler_params=pltpu.CompilerParams(
            collective_id=collective_id, has_side_effects=True, vmem_limit_bytes=VMEM_LIMIT
        ),
    )(pack, wide, down)


def forward_kernel(span, info, begin, query, key, value, mixed, lse, m_acc, l_acc, o_acc):
    rows = begin.shape[0]
    first_row, low, high = info[0], info[1], info[2]
    scale = HEAD_DIM ** (-0.5) * LOG2E
    m_acc[...] = jnp.full_like(m_acc, -1e30)
    l_acc[...] = jnp.zeros_like(l_acc)
    o_acc[...] = jnp.zeros_like(o_acc)
    places = first_row + lax.broadcasted_iota(jnp.int32, (rows, span), 0)
    offsets = lax.broadcasted_iota(jnp.int32, (rows, span), 1)

    def step(number, carry):
        base = pl.multiple_of(number * span, span)
        keys_at = base + offsets
        visible = jnp.logical_and(keys_at >= begin[...], keys_at <= places)
        for g in range(KV_HEADS):
            lanes = slice(g * HEAD_DIM, (g + 1) * HEAD_DIM)
            scores = lax.dot_general(
                query[g],
                key[pl.ds(base, span), lanes],
                (((1,), (1,)), ((), ())),
                preferred_element_type=F32,
            )
            scores = scores.reshape(GROUP, rows, span) * scale
            scores = jnp.where(visible[None], scores, -1e30).reshape(GROUP * rows, span)
            old = m_acc[g]
            new = jnp.maximum(old, jnp.max(scores, axis=-1, keepdims=True))
            weights = jnp.exp2(scores - new[:, :1])
            weights = jnp.where(
                visible[None], weights.reshape(GROUP, rows, span), 0.0
            ).reshape(GROUP * rows, span)
            fade = jnp.exp2(old - new)
            l_acc[g] = l_acc[g] * fade + jnp.sum(weights, axis=-1, keepdims=True)
            o_acc[g] = o_acc[g] * fade + jnp.dot(
                weights.astype(BF16),
                value[pl.ds(base, span), lanes],
                preferred_element_type=F32,
            )
            m_acc[g] = new
        return carry

    lax.fori_loop(low, high, step, 0)
    for g in range(KV_HEADS):
        mixed[g] = o_acc[g] / l_acc[g]
        lse[g] = m_acc[g] + jnp.log2(l_acc[g])


def call_forward(span, info, begin, query, key, value):
    stacked = query.shape[1]
    vmem = pl.BlockSpec(memory_space=pltpu.VMEM)
    return pl.pallas_call(
        functools.partial(forward_kernel, span),
        out_shape=[
            jax.ShapeDtypeStruct((KV_HEADS, stacked, HEAD_DIM), F32),
            jax.ShapeDtypeStruct((KV_HEADS, stacked, HEAD_DIM), F32),
        ],
        in_specs=[pl.BlockSpec(memory_space=pltpu.SMEM)] + [vmem] * 4,
        out_specs=[vmem, vmem],
        scratch_shapes=[pltpu.VMEM((KV_HEADS, stacked, HEAD_DIM), F32)] * 3,
        compiler_params=pltpu.CompilerParams(vmem_limit_bytes=VMEM_LIMIT),
    )(info, begin, query, key, value)


def backward_kernel(
    span, info, begin, query, key, value, mixed, lse, grad, dquery, dkeys, delta
):
    rows = begin.shape[0]
    first_row, low, high = info[0], info[1], info[2]
    scale = HEAD_DIM ** (-0.5) * LOG2E
    dquery[...] = jnp.zeros_like(dquery)
    width = KV_HEADS * HEAD_DIM
    for g in range(KV_HEADS):
        delta[g] = jnp.broadcast_to(
            jnp.sum(grad[g].astype(F32) * mixed[g], axis=-1, keepdims=True), delta.shape[1:]
        )
    places = first_row + lax.broadcasted_iota(jnp.int32, (rows, span), 0)
    offsets = lax.broadcasted_iota(jnp.int32, (rows, span), 1)

    def clear(number, carry):
        base = pl.multiple_of(number * span, span)
        dkeys[pl.ds(base, span), :] = jnp.zeros((span, dkeys.shape[1]), BF16)
        return carry

    lax.fori_loop(0, low, clear, 0)
    lax.fori_loop(high, dkeys.shape[0] // span, clear, 0)

    def step(number, carry):
        base = pl.multiple_of(number * span, span)
        keys_at = base + offsets
        visible = jnp.logical_and(keys_at >= begin[...], keys_at <= places)
        for g in range(KV_HEADS):
            lanes = slice(g * HEAD_DIM, (g + 1) * HEAD_DIM)
            key_rows = key[pl.ds(base, span), lanes]
            value_rows = value[pl.ds(base, span), lanes]
            scores = lax.dot_general(
                query[g], key_rows, (((1,), (1,)), ((), ())), preferred_element_type=F32
            )
            dprobs = lax.dot_general(
                grad[g], value_rows, (((1,), (1,)), ((), ())), preferred_element_type=F32
            )
            probs = jnp.exp2(scores * scale - lse[g][:, :1])
            probs = jnp.where(
                visible[None], probs.reshape(GROUP, rows, span), 0.0
            ).reshape(GROUP * rows, span)
            dscores = (probs * (dprobs - delta[g][:, :1])).astype(BF16)
            dquery[g] += jnp.dot(dscores, key_rows, preferred_element_type=F32)
            dkeys[pl.ds(base, span), lanes] = lax.dot_general(
                dscores, query[g], (((0,), (0,)), ((), ())), preferred_element_type=F32
            ).astype(BF16)
            dkeys[
                pl.ds(base, span), width + g * HEAD_DIM : width + (g + 1) * HEAD_DIM
            ] = lax.dot_general(
                probs.astype(BF16),
                grad[g],
                (((0,), (0,)), ((), ())),
                preferred_element_type=F32,
            ).astype(BF16)
        return carry

    lax.fori_loop(low, high, step, 0)


def call_backward(span, info, begin, query, key, value, mixed, lse, grad):
    stacked = query.shape[1]
    vmem = pl.BlockSpec(memory_space=pltpu.VMEM)
    return pl.pallas_call(
        functools.partial(backward_kernel, span),
        out_shape=[
            jax.ShapeDtypeStruct((KV_HEADS, stacked, HEAD_DIM), F32),
            jax.ShapeDtypeStruct((key.shape[0], 2 * key.shape[1]), BF16),
        ],
        in_specs=[pl.BlockSpec(memory_space=pltpu.SMEM)] + [vmem] * 7,
        out_specs=[vmem, vmem],
        scratch_shapes=[pltpu.VMEM((KV_HEADS, stacked, HEAD_DIM), F32)],
        compiler_params=pltpu.CompilerParams(vmem_limit_bytes=VMEM_LIMIT),
    )(info, begin, query, key, value, mixed, lse, grad)


def begin_of(positions, lengths):
    ends = jnp.cumsum(lengths)
    starts = ends - lengths
    inside = (positions[:, None] >= starts[None, :]) & (positions[:, None] < ends[None, :])
    return jnp.sum(jnp.where(inside, starts[None, :], 0), axis=1)


def rope_tables(places, head_size):
    half_size = head_size // 2
    frequency = ROPE_BASE ** (-2.0 * jnp.arange(half_size, dtype=F32) / head_size)
    angles = places.astype(F32)[:, None] * frequency[None, :]
    return (jnp.cos(angles), jnp.sin(angles))


def rotate(vector, cosine, sine_table, direction):
    half_size = vector.shape[-1] // 2
    front_half = vector[..., :half_size]
    back_half = vector[..., half_size:]
    cosine = cosine[:, None, :]
    sine_table = direction * sine_table[:, None, :]
    return jnp.concatenate(
        [
            front_half * cosine - back_half * sine_table,
            back_half * cosine + front_half * sine_table,
        ],
        axis=-1,
    )


def norm_back(grad_normed, normed, inverse, gain_row):
    scaled = grad_normed * gain_row
    return inverse * (scaled - normed * jnp.mean(scaled * normed, axis=-1, keepdims=True))


def dot(left, right):
    return jnp.dot(left, right, preferred_element_type=F32)


def dot_t(left, right):
    return lax.dot_general(left, right, (((1,), (1,)), ((), ())), preferred_element_type=F32)


def t_dot(left, right):
    return lax.dot_general(left, right, (((0,), (0,)), ((), ())), preferred_element_type=F32)


def column(vector, rows):
    return jnp.pad(vector, (0, rows - vector.shape[0]))[:, None]


def shards(
    tokens,
    cotangent,
    lengths,
    attn_gain,
    q_weight,
    q_bias,
    k_weight,
    k_bias,
    v_weight,
    v_bias,
    o_weight,
    mlp_gain,
    gate_weight,
    up_weight,
    down_weight,
):
    seq, fsdp = lax.axis_size("seq"), lax.axis_size("fsdp")
    devices = seq * fsdp
    depth = seq // 2
    rows, model = tokens.shape
    total = rows * devices
    key_width = KV_HEADS * HEAD_DIM
    query_width = HEADS * HEAD_DIM
    model_rows = q_weight.shape[0]
    units = gate_weight.shape[1] // seq
    first_row = lax.axis_index(AXES) * rows
    positions = first_row + jnp.arange(rows, dtype=jnp.int32)
    begin = begin_of(positions, lengths)
    cosine, sine_table = rope_tables(positions - begin, HEAD_DIM)
    score_scale = HEAD_DIM ** (-0.5)

    small = jnp.concatenate(
        [column(v, model_rows) for v in (attn_gain, q_bias, k_bias, v_bias, mlp_gain)]
        + [jnp.zeros((model_rows, 123), BF16)],
        axis=1,
    )
    pack = jnp.concatenate([q_weight, k_weight, v_weight, o_weight, small], axis=1)
    wide = jnp.stack([gate_weight, up_weight]).reshape(2, model_rows, seq, units)
    wide = wide.transpose(0, 2, 1, 3)
    pack_all, cot_all, wide_all, down_all = call_start(
        depth, 0, pack, cotangent, wide, down_weight
    )
    pack_all = pack_all.reshape(model, pack.shape[1])
    qkv_width = query_width + 2 * key_width
    w_qkv = pack_all[:, :qkv_width]
    w_out = pack_all[:, qkv_width : qkv_width + query_width]
    smalls = pack_all[:, qkv_width + query_width :].astype(F32)
    gain_one, b_query = smalls[:, 0], smalls[:, 1]
    gain_two = smalls[:, 4]
    kv_share = k_bias.shape[0]
    b_key = smalls[:, 2].reshape(devices, model_rows)[:, :kv_share].reshape(key_width)
    b_value = smalls[:, 3].reshape(devices, model_rows)[:, :kv_share].reshape(key_width)
    cot_all = cot_all.reshape(seq * rows, model)
    w_gate = wide_all[0].reshape(model, units)
    w_up = wide_all[1].reshape(model, units)
    w_down = down_all.reshape(units, model)

    inputs = tokens.astype(F32)
    inv_one = lax.rsqrt(jnp.mean(inputs * inputs, axis=-1, keepdims=True) + EPSILON)
    normed_one = inputs * inv_one
    hidden_one = (normed_one * gain_one).astype(BF16)
    lin = dot(hidden_one, w_qkv) + jnp.concatenate([b_query, b_key, b_value])
    queries = rotate(
        lin[:, :query_width].reshape(rows, HEADS, HEAD_DIM), cosine, sine_table, 1.0
    ).astype(BF16)
    queries = queries.transpose(1, 0, 2).reshape(KV_HEADS, GROUP * rows, HEAD_DIM)
    keys = rotate(
        lin[:, query_width : query_width + key_width].reshape(rows, KV_HEADS, HEAD_DIM),
        cosine,
        sine_table,
        1.0,
    ).reshape(rows, key_width)
    kv = jnp.concatenate([keys, lin[:, query_width + key_width :]], axis=1).astype(BF16)
    (kv_all,) = call_gathers(depth, 1, [True], [kv])
    kv_all = kv_all.reshape(total, 2 * key_width)
    all_keys, all_values = kv_all[:, :key_width], kv_all[:, key_width:]

    span = min(512, total)
    low = begin[0] // span
    high = (first_row + rows - 1) // span + 1
    info = jnp.stack([first_row, low, high]).astype(jnp.int32)
    begin_column = begin[:, None]
    mixed, lse = call_forward(span, info, begin_column, queries, all_keys, all_values)
    mixed_low = (
        mixed.reshape(HEADS, rows, HEAD_DIM)
        .transpose(1, 0, 2)
        .reshape(rows, query_width)
        .astype(BF16)
    )
    middle = inputs + dot(mixed_low, w_out)
    inv_two = lax.rsqrt(jnp.mean(middle * middle, axis=-1, keepdims=True) + EPSILON)
    normed_two = middle * inv_two
    hidden_two = (normed_two * gain_two).astype(BF16)

    (hidden_all,) = call_gathers(depth, 2, [False], [hidden_two])
    hidden_all = hidden_all.reshape(seq * rows, model)
    gate = dot(hidden_all, w_gate)
    up = dot(hidden_all, w_up)
    sigma = jax.nn.sigmoid(gate)
    silu = gate * sigma
    activated = (silu * up).astype(BF16)
    d_act = dot_t(cot_all, w_down)
    d_gate = (d_act * up * sigma * (1.0 + gate * (1.0 - sigma))).astype(BF16)
    d_up = (d_act * silu).astype(BF16)
    d_hidden_part = dot_t(d_gate, w_gate) + dot_t(d_up, w_up)
    out_part = dot(activated, w_down)
    shape = (depth, 2, rows, model)
    d_hidden_two, branch = call_reduces(
        depth,
        3,
        [False, False],
        [d_hidden_part.astype(BF16).reshape(shape), out_part.astype(BF16).reshape(shape)],
    )
    layer_out = (middle + branch).astype(BF16)
    gate_part = t_dot(hidden_all, d_gate).astype(BF16)
    up_part = t_dot(hidden_all, d_up).astype(BF16)
    down_part = t_dot(activated, cot_all).astype(BF16)

    gain_two_grad = jnp.sum(d_hidden_two * normed_two, axis=0)
    d_middle = cotangent.astype(F32) + norm_back(d_hidden_two, normed_two, inv_two, gain_two)

    d_branch = d_middle.astype(BF16)
    d_mixed = dot_t(d_branch, w_out).astype(BF16)
    d_mixed = (
        d_mixed.reshape(rows, HEADS, HEAD_DIM)
        .transpose(1, 0, 2)
        .reshape(KV_HEADS, GROUP * rows, HEAD_DIM)
    )
    d_query, d_kv_part = call_backward(
        span, info, begin_column, queries, all_keys, all_values, mixed, lse, d_mixed
    )
    (d_kv,) = call_reduces(
        depth, 4, [True], [d_kv_part.reshape(depth, 2, 2, 2, rows, 2 * key_width)]
    )
    d_query = d_query.reshape(HEADS, rows, HEAD_DIM).transpose(1, 0, 2)
    d_q = rotate(d_query * score_scale, cosine, sine_table, -1.0).reshape(rows, query_width)
    d_k = rotate(
        d_kv[:, :key_width].reshape(rows, KV_HEADS, HEAD_DIM) * score_scale,
        cosine,
        sine_table,
        -1.0,
    ).reshape(rows, key_width)
    d_lin = jnp.concatenate([d_q, d_k, d_kv[:, key_width:]], axis=1).astype(BF16)
    bias_grad = jnp.sum(d_lin.astype(F32), axis=0)
    d_hidden_one = dot_t(d_lin, w_qkv)
    gain_one_grad = jnp.sum(d_hidden_one * normed_one, axis=0)
    input_grad = d_middle + norm_back(d_hidden_one, normed_one, inv_one, gain_one)

    def spread(vector):
        parts = vector.reshape(devices, -1)
        return jnp.pad(parts, ((0, 0), (0, model_rows - parts.shape[1]))).reshape(model, 1)

    small_part = jnp.concatenate(
        [
            spread(gain_one_grad),
            spread(bias_grad[:query_width]),
            spread(bias_grad[query_width : query_width + key_width]),
            spread(bias_grad[query_width + key_width :]),
            spread(gain_two_grad),
            jnp.zeros((model, 123), F32),
        ],
        axis=1,
    )
    pack_part = jnp.concatenate(
        [
            t_dot(hidden_one, d_lin).astype(BF16),
            t_dot(mixed_low, d_branch).astype(BF16),
            small_part.astype(BF16),
        ],
        axis=1,
    ).reshape(depth, 2, 2, 2, model_rows, pack.shape[1])
    wide_part = jnp.stack([gate_part, up_part]).reshape(2, seq, fsdp, model_rows, units)
    down_part = down_part.reshape(fsdp, units // fsdp, model)
    pack_grad, wide_grad, down_grad = call_end(depth, 5, pack_part, wide_part, down_part)
    wide_grad = wide_grad.transpose(1, 2, 0, 3).reshape(2, model_rows, seq * units).astype(F32)
    small_grad = pack_grad[:, qkv_width + query_width :]
    return (
        layer_out,
        input_grad,
        small_grad[:, 0],
        pack_grad[:, :query_width],
        small_grad[:, 1],
        pack_grad[:, query_width : query_width + key_width],
        small_grad[:kv_share, 2],
        pack_grad[:, query_width + key_width : qkv_width],
        small_grad[:kv_share, 3],
        pack_grad[:, qkv_width : qkv_width + query_width],
        small_grad[:, 4],
        wide_grad[0],
        wide_grad[1],
        down_grad,
    )


def solution(mesh):
    matrix, vector = P(AXES, None), P(AXES)
    in_specs = (
        matrix,
        matrix,
        P(),
        vector,
        matrix,
        vector,
        matrix,
        vector,
        matrix,
        vector,
        matrix,
        vector,
        matrix,
        matrix,
        matrix,
    )
    out_specs = (
        matrix,
        matrix,
        vector,
        matrix,
        vector,
        matrix,
        vector,
        matrix,
        vector,
        matrix,
        vector,
        matrix,
        matrix,
        matrix,
    )
    return jax.shard_map(shards, mesh=mesh, in_specs=in_specs, out_specs=out_specs, check_vma=False)
```

time: 3180 us -> 729 us (0.23)
  waiting for transfers between devices: 2670 us -> 0 us
  Pallas kernels: 0 us -> 545 us
  blocking collectives: 163 us -> 0 us
  matrix products: 211 us -> 83.6 us
  other arithmetic: 61.6 us -> 24 us
    reduce_scatter x3 -> x0, waiting for transfers between devices: 1210 us -> none  [the longest x1 972 us: shards(): lax.psum_scatter(jnp.concatenate([jnp.dot(first_part, grad_query, preferr...]
    unnamed x12 -> x0, waiting for transfers between devices: 830 us -> none
    all_gather x7 -> x0, waiting for transfers between devices: 633 us -> none  [the longest x1 163 us: shards(): lax.all_gather(up_weight, ('seq', 'fsdp'), axis=0, tiled=True)]
    pallas_call x0 -> x8, Pallas kernels: none -> 545 us  [the longest x1 166 us: call_start(): pl.pallas_call(functools.partial(start_kernel, depth), out_shape=[gather_...]
    dot_general x30 -> x15, matrix products: 211 us -> 83.6 us  [the longest x5 28.7 us: dot(): return jnp.dot(left, right, preferred_element_type=F32)]
    all_gather x2 -> x0, blocking collectives: 82.3 us -> none  [the longest x1 42.7 us: shards(): lax.all_gather(v_weight, ('seq', 'fsdp'), axis=0, tiled=True)]
    unnamed x2 -> x0, blocking collectives: 81.1 us -> none
    concatenate x1 -> x2, other arithmetic: 43.5 us -> 0.67 us  [the longest x1 0.67 us: shards(): jnp.concatenate([keys, lin[:, query_width + key_width:]], axis=1)]
  transfers between devices with their start and end apart: 11 -> 0, of which waited for: 11 -> 0; matrix products, arithmetic and copies ran while one was open for 7% -> 0% of each run, Pallas kernels for 0% -> 0%
where the time goes in v1:
time: 729 us; the launch traced here: 726 us
  Pallas kernels  545 us (75%)
  matrix products  83.6 us (11%)
  local copies, waits for them, and re-layouts  72.2 us (10%)
  other arithmetic  24 us (3%)
    pallas_call x1, Pallas kernels, call_start(): pl.pallas_call(functools.partial(start_kernel, depth), out_shape=[gather_...  166 us
    pallas_call x2, Pallas kernels, call_reduces(): pl.pallas_call(kernel, out_shape=[jax.ShapeDtypeStruct(block, F32) for bl...  137 us
    pallas_call x1, Pallas kernels, call_end(): pl.pallas_call(functools.partial(end_kernel, depth, (block, wide_block, d...  131 us
    pallas_call x2, Pallas kernels, call_gathers(): pl.pallas_call(kernel, out_shape=[gather_shape(depth, wide, own) for wide...  84.8 us
    dot_general x5, matrix products, dot(): return jnp.dot(left, right, preferred_element_type=F32)  28.7 us
    dot_general x5, matrix products, t_dot(): lax.dot_general(left, right, (((0,), (0,)), ((), ())), preferred_element_...  28.3 us
    dot_general x5, matrix products, dot_t(): lax.dot_general(left, right, (((1,), (1,)), ((), ())), preferred_element_...  26.5 us
    concatenate x1, local copies, waits for them, and re-layouts, shards(): jnp.concatenate([t_dot(hidden_one, d_lin).astype(BF16), t_dot(mixed_low,...  18.1 us

profile of v1, /device:TPU:0, one launch (start us, length us, event | category | flops | bytes accessed | tf_op | source)
XLA Modules:
  0.0 726.1 jit_solution(3795237414506032380)
XLA Ops:
  15.4 165.9 %shard_map.254 = (bf16[4,2,2,2,48,3712]{5,4,3,2,1,0:T(8,128)(2,1)}, bf16[4,2,128,1536]{3,2,1,0:T(8,128)(2,1)}, bf16[2,8,4,48,1120]{4,3,2,1,0:T(8,128)(2,1)}, bf16[4,280,1536]{2,1,0:T(8,128)(2,1)}) custom-call(bf16[48,3712]{1,0:T(8,128)(2,1)} %concatenate.38.refs_0_, bf16[128,1536]{1,0:T(8,128)(2,1)} %refs_1_.1, ...), custom_call_target="tpu_custom_call" | custom-call | tf_op jit(solution)/shard_map/pallas_call | solution.py:404
  190.2 27.8 %shard_map.255 = bf16[4,2,2,2,128,512]{5,4,3,2,1,0:T(8,128)(2,1)} custom-call(bf16[128,512]{1,0:T(8,128)(2,1)} %pad_maximum_fusion.3.refs_0_), custom_call_target="tpu_custom_call" | custom-call | tf_op jit(solution)/shard_map/pallas_call | solution.py:279
  218.1 4.5 fusion.35
  222.6 17.6 %shard_map.256 = (f32[2,768,128]{2,1,0:T(8,128)}, f32[2,768,128]{2,1,0:T(8,128)}) custom-call(s32[3]{0:T(128)} %pad_add_fusion.info, s32[128,1]{1,0:T(8,128)} %copy.85.begin, bf16[2,768,128]{2,1,0:T(8,128)(2,1)} %bitcast.95, bf16[4096,256]{1,0:T(8,128)(2,1)} %get-tuple-element.60.key, bf16[4096,256]{1,0:T(8,128)(2,1)} %get-tuple-element.59.value), custom_call_target="tpu_custom_call" | custom-call | tf_op jit(solution)/shard_map/pallas_call | solution.py:856
  249.4 56.9 %shard_map.257 = bf16[4,2,128,1536]{3,2,1,0:T(8,128)(2,1)} custom-call(bf16[128,1536]{1,0:T(8,128)(2,1)} %multiply_convert_fusion.3.refs_0_), custom_call_target="tpu_custom_call" | custom-call | tf_op jit(solution)/shard_map/pallas_call | solution.py:279
  308.3 5.5 fusion.41
  313.8 5.4 fusion.40
  319.2 10.0 %multiply_convert_fusion = (bf16[1024,1120]{0,1:T(8,128)(2,1)}, bf16[1024,1120]{0,1:T(8,128)(2,1)}, bf16[1024,1120]{0,1:T(8,128)(2,1)}) fusion(f32[1024,1120]{0,1:T(8,128)} %fusion.41, f32[1024,1120]{0,1:T(8,128)} %fusion.40, bf16[1024,1536]{1,0:T(8,128)(2,1)S(1)} %bitcast.100, bf16[1536,1120]{1,0:T(8,128)(2,1)S(1)} %bitcast.91), kind=kOutput, calls=%fused_computation.11 | convolution fusion | flops 3540418560 | bytes 22642688 | tf_op jit(solution)/shard_map/dot_general | solution.py:979
  329.1 6.1 fusion.42
  335.3 5.9 add_convert_fusion
  341.2 6.0 convolution_convert_fusion.5
  347.2 90.7 %shard_map.258 = (f32[128,1536]{1,0:T(8,128)}, f32[128,1536]{1,0:T(8,128)}) custom-call(bf16[4,2,128,1536]{3,2,1,0:T(8,128)(2,1)} %bitcast.102, bf16[4,2,128,1536]{3,2,1,0:T(8,128)(2,1)} %bitcast.103), custom_call_target="tpu_custom_call" | custom-call | tf_op jit(solution)/shard_map/pallas_call | solution.py:642
  446.9 8.0 %shard_map.259 = (f32[2,768,128]{2,1,0:T(8,128)}, bf16[4096,512]{1,0:T(8,128)(2,1)}) custom-call(s32[3]{0:T(128)} %pad_add_fusion.info, s32[128,1]{1,0:T(8,128)} %copy.85.begin, bf16[2,768,128]{2,1,0:T(8,128)(2,1)} %bitcast.96, bf16[4096,256]{1,0:T(8,128)(2,1)} %get-tuple-element.60.key, bf16[4096,256]{1,0:T(8,128)(2,1)} %get-tuple-element.59.value, ...), custom_call_target="tpu_custom_call" | custom-call | tf_op jit(solution)/shard_map/pallas_call | solution.py:931
  454.9 46.3 %shard_map.260 = f32[128,512]{1,0:T(8,128)} custom-call(bf16[4,2,2,2,128,512]{5,4,3,2,1,0:T(8,128)(2,1)} %bitcast.87), custom_call_target="tpu_custom_call" | custom-call | tf_op jit(solution)/shard_map/pallas_call | solution.py:642
  505.7 5.1 fusion.27
  512.0 4.6 convolution_convert_fusion.3
  526.0 18.1 %concatenate.46 = bf16[1536,3712]{1,0:T(8,128)(2,1)} concatenate(bf16[1536,2048]{1,0:T(8,128)(2,1)} %convolution_convert_fusion.3, bf16[1536,1536]{1,0:T(8,128)(2,1)} %convolution_convert_fusion.4, bf16[1536,1]{1,0:T(8,128)(2,1)S(1)} %reshape.327, bf16[1536,1]{1,0:T(8,128)(2,1)} %reshape.328, bf16[1536,1]{1,0:T(8,128)(2,1)} %reshape.329, bf16[1536,1]{1,0:T(8,128)(2,1)} %reshape.330, ...), dimensions={1} | concatenate | bytes 22806528 | tf_op jit(solution)/shard_map/concatenate | solution.py:1158
  544.1 6.9 convolution_convert_fusion
  551.0 4.3 copy.101
  555.3 8.2 %convolution_convert_fusion.1 = bf16[1536,1120]{0,1:T(8,128)(2,1)} fusion(bf16[1024,1120]{0,1:T(8,128)(2,1)} %get-tuple-element.55, bf16[1024,1536]{1,0:T(8,128)(2,1)} %bitcast.98), kind=kOutput, calls=%fused_computation.1 | convolution fusion | flops 3524935680 | bytes 8880128 | tf_op jit(solution)/shard_map/dot_general | solution.py:987
  563.5 5.7 copy.100
  569.2 5.9 pad_maximum_fusion.refs_1_
  575.0 5.2 convolution_convert_fusion.2
  580.2 131.4 %shard_map.261 = (f32[48,3712]{1,0:T(8,128)}, bf16[8,2,48,1120]{3,2,1,0:T(8,128)(2,1)}, f32[280,1536]{1,0:T(8,128)}) custom-call(bf16[4,2,2,2,48,3712]{5,4,3,2,1,0:T(8,128)(2,1)} %bitcast.81, bf16[2,8,4,48,1120]{4,3,2,1,0:T(8,128)(2,1)} %pad_maximum_fusion.refs_1_, bf16[4,280,1536]{2,1,0:T(8,128)(2,1)} %bitcast.97), custom_call_target="tpu_custom_call" | custom-call | tf_op jit(solution)/shard_map/pallas_call | solution.py:791
  (136 shorter events, 72.5 us)
Async XLA Ops:
  0.6 11.7 %copy-start.9 = (bf16[48,8960]{1,0:T(8,128)(2,1)S(1)}, bf16[48,8960]{1,0:T(8,128)(2,1)}, u32[]{:S(2)}) copy-start(bf16[48,8960]{1,0:T(8,128)(2,1)} %param.27) | copy-start | bytes 2580484
  15.4 167.7 %copy-start.2 = (bf16[128,1536]{1,0:T(8,128)(2,1)S(1)}, bf16[128,1536]{1,0:T(8,128)(2,1)}, u32[]{:S(2)}) copy-start(bf16[128,1536]{1,0:T(8,128)(2,1)} %param.15) | copy-start | bytes 1179652
  240.2 66.2 %slice-start = ((s8[7077888]{0:T(1024)(128)(4,1)}), s8[2883584]{0:T(1024)(128)(4,1)S(1)}, s32[]{:S(2)}) async-start(s8[7077888]{0:T(1024)(128)(4,1)} %bitcast.85), calls=%async_computation | async-start | bytes 5767168
  244.2 62.2 %slice-start.1 = ((s8[7077888]{0:T(1024)(128)(4,1)}), s8[4194304]{0:T(1024)(128)(4,1)S(1)}, s32[]{:S(2)}) async-start(s8[7077888]{0:T(1024)(128)(4,1)} %bitcast.85), calls=%async_computation.1 | async-start | bytes 8388608
  247.7 0.9 copy-start
  306.4 1.9 copy-start.3
  308.3 5.5 copy-start.10
  308.3 5.5 copy-start.11
  313.8 5.4 copy-start.4
  329.1 6.1 copy-start.15
  335.3 5.9 copy-start.13
  347.2 90.7 %copy-start.1 = (f32[128,1536]{1,0:T(8,128)S(1)}, f32[128,1536]{1,0:T(8,128)}, u32[]{:S(2)}) copy-start(f32[128,1536]{1,0:T(8,128)} %copy-done) | copy-start | bytes 2359300
  347.2 92.1 %copy-start.8 = (bf16[128,1536]{1,0:T(8,128)(2,1)S(1)}, bf16[128,1536]{1,0:T(8,128)(2,1)}, u32[]{:S(2)}) copy-start(bf16[128,1536]{1,0:T(8,128)(2,1)} %refs_1_.1) | copy-start | bytes 1179652
  512.0 4.6 copy-start.6
  526.0 18.1 %copy-start.5 = (bf16[4,2,128,1536]{3,2,1,0:T(8,128)(2,1)S(1)}, bf16[4,2,128,1536]{3,2,1,0:T(8,128)(2,1)}, u32[]{:S(2)}) copy-start(bf16[4,2,128,1536]{3,2,1,0:T(8,128)(2,1)} %shard_map.257) | copy-start | bytes 9437188
  569.2 5.9 copy-start.12
  569.2 5.9 copy-start.14
  722.9 1.7 copy-start.7

commit v2 on v1

--- a/solution.py
+++ b/solution.py
@@ -16,6 +16,7 @@
 LOG2E = 1.4426950408889634
 AXES = ("seq", "fsdp")
 VMEM_LIMIT = 56 << 20
+VMEM_JOINED = 60 << 20
 F32 = jnp.float32
 BF16 = jnp.bfloat16
 DMA = pltpu.SemaphoreType.DMA
@@ -419,10 +420,19 @@
 
 
 class Reduce:
-    def __init__(self, place, wide, rows, own, out, buffers, sems):
+    def __init__(self, place, wide, rows, own, out, buffers, sems, near=None, causal=False):
         self.place, self.wide, self.rows = place, wide, rows
         self.own, self.out, self.buffers, self.sems = own, out, buffers, sems
+        self.near = near
+        self.causal = causal
         self.sent = []
+
+    def wave(self, k):
+        waves = self.place.wave(k)
+        return waves[:1] if self.causal else waves
+
+    def near_block(self, zi):
+        return self.own.at[zi, self.place.x] if self.near is None else self.near.at[zi]
 
     @staticmethod
     def scratch(depth, wide, block):
@@ -448,7 +458,7 @@
         place = self.place
         c_send, c_recv = self.sems[4:6]
         got = self.buffers[2]
-        for zi, ok in place.wave(k):
+        for zi, ok in self.wave(k):
             for x in range(2):
                 for y in range(2):
                     slot = 4 * zi + 2 * x + y
@@ -465,7 +475,7 @@
         place = self.place
         c_send, c_recv, b_send, b_recv = self.sems[4:8]
         got, next_ = self.buffers[2:4]
-        for zi, ok in place.wave(k):
+        for zi, ok in self.wave(k):
 
             def body(zi=zi):
                 for j in (1, 0):
@@ -502,7 +512,7 @@
         place = self.place
         a_send, a_recv = self.sems[0:2]
         got = self.buffers[0]
-        for zi, ok in place.wave(k):
+        for zi, ok in self.wave(k):
             if self.wide:
                 b_send, b_recv = self.sems[6:8]
                 before, held = self.buffers[2:4]
@@ -539,7 +549,7 @@
         place, depth = self.place, self.place.depth
         a_send, a_recv, z_send, z_recv = self.sems[0:4]
         held, line = self.buffers[0:2]
-        for side, (zi, ok) in enumerate(place.wave(k)):
+        for side, (zi, ok) in enumerate(self.wave(k)):
             block = held.at[zi]
 
             def body(zi=zi, side=side, block=block):
@@ -547,7 +557,7 @@
                 if self.wide:
                     add_into(block, self.buffers[3].at[zi, 0], self.rows)
                 else:
-                    add_into(block, self.own.at[zi, place.x], self.rows)
+                    add_into(block, self.near_block(zi), self.rows)
 
                 def more(direction):
                     slot = direction * depth + zi
@@ -561,7 +571,8 @@
                     remote(block, there, z_send.at[slot], z_recv.at[slot], to).start()
 
                 if k == 0:
-                    pl.when(place.down)(functools.partial(more, 0))
+                    if not self.causal:
+                        pl.when(place.down)(functools.partial(more, 0))
                     pl.when(place.up)(functools.partial(more, 1))
                 elif side == 0:
                     pl.when(place.up)(functools.partial(more, 1))
@@ -941,6 +952,919 @@
     )(info, begin, query, key, value, mixed, lse, grad)
 
 
+class Exchange:
+    def __init__(self, place, own, out, sems):
+        self.place, self.own, self.out, self.sems = place, own, out, sems
+        self.count = 2 * place.depth
+        self.sent = []
+        self.y_f = place.f + 2 - 4 * place.y
+        self.c_f = place.f + 1 - 2 * place.c
+        self.yc_f = self.y_f + 1 - 2 * place.c
+
+    @staticmethod
+    def semaphores(depth):
+        count = 2 * depth
+        return [
+            DMA((1,)),
+            DMA((count,)),
+            DMA((count,)),
+            DMA((count,)),
+            DMA((count,)),
+            DMA((2 * count,)),
+            DMA((2 * count,)),
+        ]
+
+    def send(self, block, send_sem, recv_sem, device, source=None):
+        copy = remote(block if source is None else source, block, send_sem, recv_sem, device)
+        copy.start()
+        self.sent.append(copy)
+
+    def block(self, offset, owner):
+        origin = lax.rem(self.place.s + self.count - offset, self.count)
+        return self.out.at[:, origin, owner]
+
+    def landed(self, block, recv_sem):
+        remote(block, block, self.sems[1].at[0], recv_sem, self.place.flip_c()).wait_recv()
+
+    def local(self):
+        return pltpu.make_async_copy(
+            self.own.at[:, self.place.s], self.block(0, self.place.f), self.sems[0].at[0]
+        )
+
+    def depart(self, offset):
+        place = self.place
+        to = lax.rem(place.s + offset, self.count)
+        self.send(
+            self.block(0, place.f),
+            self.sems[1].at[offset],
+            self.sems[2].at[offset],
+            (to, place.f),
+            self.own.at[:, to],
+        )
+
+    def onward(self, offset):
+        place = self.place
+        block = self.block(offset, place.f)
+        if offset > 0:
+            self.landed(block, self.sems[2].at[offset])
+        self.send(block, self.sems[3].at[offset], self.sems[4].at[offset], place.flip_y())
+        slot = 2 * offset
+        self.send(block, self.sems[5].at[slot], self.sems[6].at[slot], place.flip_c())
+
+    def sideways(self, offset):
+        block = self.block(offset, self.y_f)
+        self.landed(block, self.sems[4].at[offset])
+        slot = 2 * offset + 1
+        self.send(block, self.sems[5].at[slot], self.sems[6].at[slot], self.place.flip_c())
+
+    def last(self, offset):
+        self.landed(self.block(offset, self.c_f), self.sems[6].at[2 * offset])
+        self.landed(self.block(offset, self.yc_f), self.sems[6].at[2 * offset + 1])
+
+    def settle(self):
+        for copy in self.sent:
+            copy.wait_send()
+
+
+class Quarter:
+    def __init__(self, place, own, out, sems):
+        self.place, self.own, self.out, self.sems = place, own, out, sems
+        self.sent = []
+
+    @staticmethod
+    def semaphores():
+        return [DMA((1,)), DMA((3,)), DMA((3,))]
+
+    def local(self):
+        return pltpu.make_async_copy(self.own, self.out.at[self.place.f], self.sems[0].at[0])
+
+    def send(self, source, block, slot, device):
+        copy = remote(source, block, self.sems[1].at[slot], self.sems[2].at[slot], device)
+        copy.start()
+        self.sent.append(copy)
+
+    def depart(self):
+        place = self.place
+        self.send(self.own, self.out.at[place.f], 0, place.flip_y())
+        self.send(self.own, self.out.at[place.f], 1, place.flip_c())
+
+    def landed(self, owner, slot):
+        block = self.out.at[owner]
+        remote(block, block, self.sems[1].at[0], self.sems[2].at[slot], self.place.flip_c()).wait_recv()
+
+    def sideways(self):
+        place = self.place
+        y_f = place.f + 2 - 4 * place.y
+        self.landed(y_f, 0)
+        self.send(self.out.at[y_f], self.out.at[y_f], 2, place.flip_c())
+
+    def last(self):
+        place = self.place
+        self.landed(place.f + 1 - 2 * place.c, 1)
+        self.landed(place.f + 2 - 4 * place.y + 1 - 2 * place.c, 2)
+
+    def settle(self):
+        for copy in self.sent:
+            copy.wait_send()
+
+
+def stage(gather, step):
+    depth = gather.place.depth
+    if step < depth:
+        gather.arrive(step)
+    if 0 <= step - 1 < depth:
+        gather.across(step - 1)
+    if gather.wide and 0 <= step - 2 < depth:
+        gather.hand(step - 2)
+    if gather.wide and 0 <= step - 3 < depth:
+        gather.take(step - 3)
+
+
+def turned(vector, cosine, sine):
+    return vector * cosine + pltpu.roll(vector, HEAD_DIM // 2, 1) * sine
+
+
+HEAD_INS = 9
+HEAD_OUTS = 13
+
+
+def head_kernel(depth, *refs):
+    (pack, o_own, cot, wide, down, tokens, cosine, sine, begin) = refs[:HEAD_INS]
+    (
+        pack_out,
+        o_out,
+        kv_out,
+        cot_out,
+        wide_out,
+        down_out,
+        hidden_out,
+        queries,
+        mixed,
+        lse,
+        middle,
+        hidden_one,
+        mixed_low,
+    ) = refs[HEAD_INS : HEAD_INS + HEAD_OUTS]
+    vectors = refs[HEAD_INS + HEAD_OUTS]
+    rest = refs[HEAD_INS + HEAD_OUTS + 1 :]
+    pack_all, o_all, kv_all, kv_own, hidden_two, lin, m_acc, l_acc, o_acc = rest[:9]
+    sems = list(rest[9:])
+
+    def take(count):
+        taken = sems[:count]
+        del sems[:count]
+        return taken
+
+    wide_need = len(Gather.semaphores(depth, True))
+    line_need = len(Gather.semaphores(depth, False))
+    count = 2 * depth
+    devices = 4 * count
+    rows, model = tokens.shape
+    query_width, key_width = HEADS * HEAD_DIM, KV_HEADS * HEAD_DIM
+    qkv_width = query_width + 2 * key_width
+
+    place = Place(depth)
+    greet(place, [(lax.rem(place.s + offset, count), place.f) for offset in range(1, count)])
+    g_pack = Gather(place, True, pack, pack_all, take(wide_need))
+    g_o = Gather(place, True, o_own, o_all, take(wide_need))
+    g_kv = Gather(place, True, kv_own, kv_all, take(wide_need))
+    g_cot = Gather(place, False, cot, cot_out, take(line_need))
+    g_hidden = Gather(place, False, hidden_two, hidden_out, take(line_need))
+    x_wide = Exchange(place, wide, wide_out, take(len(Exchange.semaphores(depth))))
+    x_down = Quarter(place, down, down_out, take(len(Quarter.semaphores())))
+    (out_sem,) = take(1)
+
+    g_pack.arrive(0)
+    locals_ = [job.local() for job in (g_pack, g_o, g_cot, x_wide, x_down)]
+    for copy in locals_:
+        copy.start()
+    inputs = tokens[...].astype(F32)
+    inv_one = lax.rsqrt(jnp.mean(inputs * inputs, axis=-1, keepdims=True) + EPSILON)
+    share = key_width // devices
+    chosen = lax.broadcasted_iota(jnp.int32, (model, key_width), 1)
+    chosen = lax.div(chosen, share) * (model // devices) + lax.rem(chosen, share)
+    chosen = (lax.broadcasted_iota(jnp.int32, (model, key_width), 0) == chosen).astype(BF16)
+    for copy in locals_:
+        copy.wait()
+    for step in range(1, depth):
+        stage(g_pack, step)
+    for offset in range(1, count):
+        x_wide.depart(offset)
+    for step in range(depth, depth + 3):
+        stage(g_pack, step)
+        if step == depth:
+            x_down.depart()
+
+    small = pack_all[:, :, :, :, :, qkv_width:].reshape(model, 128).astype(F32).T
+    vectors[...] = small[:8]
+    spread = jnp.dot(small[:8].astype(BF16), chosen, preferred_element_type=F32)
+    hidden_one[...] = (inputs * inv_one * small[0:1]).astype(BF16)
+    part = model // depth
+    for zi in range(depth):
+        weights = pack_all[zi][:, :, :, :, :qkv_width].reshape(part, qkv_width)
+        term = jnp.dot(
+            hidden_one[:, zi * part : (zi + 1) * part], weights, preferred_element_type=F32
+        )
+        if zi == 0:
+            lin[...] = term
+        else:
+            lin[...] += term
+    for g in range(KV_HEADS):
+        lanes = slice(query_width + g * HEAD_DIM, query_width + (g + 1) * HEAD_DIM)
+        own = slice(g * HEAD_DIM, (g + 1) * HEAD_DIM)
+        head = lin[:, lanes] + spread[2:3, own]
+        kv_own[:, own] = turned(head, cosine[...], sine[...]).astype(BF16)
+    values = lin[:, query_width + key_width :] + spread[3:4]
+    kv_own[:, key_width:] = values.astype(BF16)
+    kv_local = g_kv.local()
+    kv_local.start()
+    g_kv.arrive(0)
+    g_o.arrive(0)
+    for h in range(HEADS):
+        lanes = slice(h * HEAD_DIM, (h + 1) * HEAD_DIM)
+        at = (h % GROUP) * rows
+        head = lin[:, lanes] + small[1:2, lanes]
+        queries[h // GROUP, at : at + rows, :] = turned(head, cosine[...], sine[...]).astype(BF16)
+    kv_local.wait()
+    for step in range(1, depth + 3):
+        stage(g_kv, step)
+        if step >= 2:
+            x_wide.onward(step - 2)
+    done_onward = depth + 1
+    for step in range(1, depth):
+        stage(g_o, step)
+    g_cot.arrive(0)
+
+    span = 4 * rows
+    scale = HEAD_DIM ** (-0.5) * LOG2E
+    m_acc[...] = jnp.full_like(m_acc, -1e30)
+    l_acc[...] = jnp.zeros_like(l_acc)
+    o_acc[...] = jnp.zeros_like(o_acc)
+    first_row = (place.s * 4 + place.f) * rows
+    places = first_row + lax.broadcasted_iota(jnp.int32, (rows, span), 0)
+    offsets = lax.broadcasted_iota(jnp.int32, (rows, span), 1)
+
+    def attend(number, carry):
+        keys_at = number * span + offsets
+        visible = jnp.logical_and(keys_at >= begin[...], keys_at <= places)
+        block = kv_all.at[lax.div(number, 2), lax.rem(number, 2)]
+        for g in range(KV_HEADS):
+            key = block[:, :, :, g * HEAD_DIM : (g + 1) * HEAD_DIM].reshape(span, HEAD_DIM)
+            value = block[
+                :, :, :, key_width + g * HEAD_DIM : key_width + (g + 1) * HEAD_DIM
+            ].reshape(span, HEAD_DIM)
+            scores = lax.dot_general(
+                queries[g], key, (((1,), (1,)), ((), ())), preferred_element_type=F32
+            )
+            scores = scores.reshape(GROUP, rows, span) * scale
+            scores = jnp.where(visible[None], scores, -1e30).reshape(GROUP * rows, span)
+            old = m_acc[g]
+            new = jnp.maximum(old, jnp.max(scores, axis=-1, keepdims=True))
+            weights = jnp.exp2(scores - new[:, :1])
+            weights = jnp.where(
+                visible[None], weights.reshape(GROUP, rows, span), 0.0
+            ).reshape(GROUP * rows, span)
+            fade = jnp.exp2(old - new)
+            l_acc[g] = l_acc[g] * fade + jnp.sum(weights, axis=-1, keepdims=True)
+            o_acc[g] = o_acc[g] * fade + jnp.dot(
+                weights.astype(BF16), value, preferred_element_type=F32
+            )
+            m_acc[g] = new
+        return carry
+
+    pieces = 4
+    for piece in range(pieces):
+        low, high = piece * count // pieces, (piece + 1) * count // pieces
+        lax.fori_loop(
+            jnp.minimum(low, place.s + 1), jnp.minimum(high, place.s + 1), attend, 0
+        )
+        if depth + piece < depth + 3:
+            stage(g_o, depth + piece)
+        if piece > 0:
+            stage(g_cot, piece)
+        if done_onward < count:
+            x_wide.onward(done_onward)
+            done_onward += 1
+    for g in range(KV_HEADS):
+        total = o_acc[g] / l_acc[g]
+        mixed[g] = total
+        lse[g] = m_acc[g] + jnp.log2(l_acc[g])
+        for j in range(GROUP):
+            lanes = slice((g * GROUP + j) * HEAD_DIM, (g * GROUP + j + 1) * HEAD_DIM)
+            mixed_low[:, lanes] = total[j * rows : (j + 1) * rows].astype(BF16)
+    after = inputs
+    for zi in range(depth):
+        after = after + jnp.dot(
+            mixed_low[:, zi * part : (zi + 1) * part],
+            o_all[zi].reshape(part, model),
+            preferred_element_type=F32,
+        )
+    middle[...] = after
+    inv_two = lax.rsqrt(jnp.mean(after * after, axis=-1, keepdims=True) + EPSILON)
+    hidden_two[...] = (after * inv_two * small[4:5]).astype(BF16)
+    hidden_local = g_hidden.local()
+    hidden_local.start()
+    g_hidden.arrive(0)
+
+    keeps = []
+    for number, (source, target) in enumerate(
+        ((pack_all, pack_out), (o_all, o_out), (kv_all, kv_out))
+    ):
+        copy = pltpu.make_async_copy(source, target, out_sem.at[number])
+        copy.start()
+        keeps.append(copy)
+    while done_onward < count:
+        x_wide.onward(done_onward)
+        done_onward += 1
+    hidden_local.wait()
+    sideways = 0
+    for step in range(1, depth + 1):
+        stage(g_hidden, step)
+        if step == 1:
+            for later in range(pieces, depth + 1):
+                stage(g_cot, later)
+            x_down.sideways()
+        while sideways < step * count // depth:
+            x_wide.sideways(sideways)
+            sideways += 1
+    for offset in range(count):
+        x_wide.last(offset)
+    x_down.last()
+    for copy in keeps:
+        copy.wait()
+    for job in (g_pack, g_o, g_kv, g_cot, g_hidden, x_wide, x_down):
+        job.settle()
+
+
+def call_head(depth, collective_id, pack, o_own, cot, wide, down, tokens, cosine, sine, begin):
+    count = 2 * depth
+    rows, model = tokens.shape
+    key_width = KV_HEADS * HEAD_DIM
+    stacked = GROUP * rows
+    kv_own = jax.ShapeDtypeStruct((rows, 2 * key_width), BF16)
+    any_, vmem = pl.BlockSpec(memory_space=pl.ANY), pl.BlockSpec(memory_space=pltpu.VMEM)
+    heads = (KV_HEADS, stacked, HEAD_DIM)
+    outs = [
+        gather_shape(depth, True, pack),
+        gather_shape(depth, True, o_own),
+        gather_shape(depth, True, kv_own),
+        gather_shape(depth, False, cot),
+        jax.ShapeDtypeStruct((2, count, 4) + wide.shape[2:], BF16),
+        jax.ShapeDtypeStruct((4,) + down.shape, BF16),
+        gather_shape(depth, False, tokens),
+        jax.ShapeDtypeStruct(heads, BF16),
+        jax.ShapeDtypeStruct(heads, F32),
+        jax.ShapeDtypeStruct(heads, F32),
+        jax.ShapeDtypeStruct((rows, model), F32),
+        jax.ShapeDtypeStruct((rows, model), BF16),
+        jax.ShapeDtypeStruct((rows, model), BF16),
+        jax.ShapeDtypeStruct((8, model), F32),
+    ]
+    scratch = [pltpu.VMEM(out.shape, BF16) for out in outs[:3]]
+    scratch += [
+        pltpu.VMEM(kv_own.shape, BF16),
+        pltpu.VMEM((rows, model), BF16),
+        pltpu.VMEM((rows, (HEADS + 2 * KV_HEADS) * HEAD_DIM), F32),
+        pltpu.VMEM(heads, F32),
+        pltpu.VMEM(heads, F32),
+        pltpu.VMEM(heads, F32),
+    ]
+    scratch += Gather.semaphores(depth, True) * 3 + Gather.semaphores(depth, False) * 2
+    scratch += Exchange.semaphores(depth) + Quarter.semaphores() + [DMA((3,))]
+    return pl.pallas_call(
+        functools.partial(head_kernel, depth),
+        out_shape=outs,
+        in_specs=[any_] * 5 + [vmem] * 4,
+        out_specs=[any_] * 7 + [vmem] * 7,
+        scratch_shapes=scratch,
+        compiler_params=pltpu.CompilerParams(
+            collective_id=collective_id, has_side_effects=True, vmem_limit_bytes=VMEM_LIMIT
+        ),
+    )(pack, o_own, cot, wide, down, tokens, cosine, sine, begin)
+
+
+def t_mul(left, right):
+    return lax.dot_general(left, right, (((0,), (0,)), ((), ())), preferred_element_type=F32)
+
+
+def mul_t(left, right):
+    return lax.dot_general(left, right, (((1,), (1,)), ((), ())), preferred_element_type=F32)
+
+
+def middle_kernel(depth, *refs):
+    (dh_part, out_part, hidden_all, cot_all, act, d_gate, d_up, o_own) = refs[:8]
+    (middle, cotangent, vectors) = refs[8:11]
+    (layer_out, d_middle, d_mixed, d_branch, gain_two, down_out, wide_out) = refs[11:18]
+    (dh_near, out_near, dh_sum, out_sum, wide_tokens, left_tokens, right_tokens) = refs[18:25]
+    (w_part, w_core, w_y, d_part, d_core, d_y, o_all) = refs[25:32]
+    rest = list(refs[32:])
+
+    def take(count):
+        taken = rest[:count]
+        del rest[:count]
+        return taken
+
+    count = 2 * depth
+    rows, model = middle.shape
+    units = act.shape[1]
+    part = model // depth
+    block = (rows, model)
+    buffers, sems = Reduce.scratch(depth, False, block)
+    place = Place(depth)
+    greet(place)
+    r_dh = Reduce(
+        place, False, rows, dh_part, dh_sum, take(len(buffers)), take(len(sems)), dh_near
+    )
+    r_out = Reduce(
+        place, False, rows, out_part, out_sum, take(len(buffers)), take(len(sems)), out_near
+    )
+    load_sem, wc_send, wc_recv, wy_send, wy_recv, dc_send, dc_recv, dy_send, dy_recv = take(9)
+    sent = []
+
+    def send(src, dst, send_sem, recv_sem, device):
+        copy = remote(src, dst, send_sem, recv_sem, device)
+        copy.start()
+        sent.append(copy)
+
+    def landed(ref, recv_sem):
+        remote(ref, ref, wc_send.at[0], recv_sem, place.flip_c()).wait_recv()
+
+    order = list(range(depth - 1, -1, -1))
+    for k in order:
+        r_dh.over_first(k)
+    loads = [
+        pltpu.make_async_copy(source, target, load_sem.at[number])
+        for number, (source, target) in enumerate(
+            (
+                (hidden_all, wide_tokens),
+                (d_gate, left_tokens),
+                (d_up, right_tokens),
+                (dh_part.at[:, place.x], dh_near),
+                (out_part.at[:, place.x], out_near),
+                (o_own, o_all),
+            )
+        )
+    ]
+    for copy in loads:
+        copy.start()
+    for k in order:
+        r_out.over_first(k)
+    mine_y, other_y = place.y, 1 - place.y
+    wide_rows = w_part.shape[-2]
+
+    def wide_chunk(k):
+        lanes = slice(k * part, (k + 1) * part)
+        tokens = wide_tokens[:, :, :, lanes].reshape(count * rows, part)
+        for side, grad in enumerate((left_tokens, right_tokens)):
+            term = t_mul(tokens, grad[...]).astype(BF16)
+            w_part[side, 2 * k : 2 * k + 2] = term.reshape(2, 2, 2, wide_rows, units)
+        for to in (2 * k, 2 * k + 1):
+            for y in range(2):
+                send(
+                    w_part.at[:, to, y, 1 - place.c],
+                    w_core.at[y, to],
+                    wc_send.at[2 * to + y],
+                    wc_recv.at[2 * to + y],
+                    place.flip_c(),
+                )
+
+    def wide_cores(to):
+        for y in (other_y, mine_y):
+            landed(w_core.at[y, to], wc_recv.at[2 * to + y])
+            for side in range(2):
+                add_into(
+                    w_core.at[y, to, side], w_part.at[side, to, y, place.c], wide_rows
+                )
+            if y is other_y:
+                send(w_core.at[y, to], w_y.at[to], wy_send.at[to], wy_recv.at[to], place.flip_y())
+
+    def wide_across(to):
+        landed(w_y.at[to], wy_recv.at[to])
+        for side in range(2):
+            wide_out[to, side] = (
+                w_y[to, side].astype(F32) + w_core[mine_y, to, side].astype(F32)
+            ).astype(BF16)
+
+    for copy in loads[:3]:
+        copy.wait()
+    for k in range(depth):
+        wide_chunk(k)
+        if k == 1:
+            for copy in loads[3:5]:
+                copy.wait()
+        if k >= 1:
+            for to in (2 * k - 2, 2 * k - 1):
+                wide_cores(to)
+            r_dh.along(order[k - 1])
+    second = [
+        pltpu.make_async_copy(cot_all, wide_tokens, load_sem.at[0]),
+        pltpu.make_async_copy(act, left_tokens, load_sem.at[1]),
+    ]
+    for copy in second:
+        copy.start()
+    for to in (count - 2, count - 1):
+        wide_cores(to)
+    loads[5].wait()
+    for copy in second:
+        copy.wait()
+    down_rows = d_part.shape[1]
+    for k in range(depth):
+        lanes = slice(k * part, (k + 1) * part)
+        tokens = wide_tokens[:, :, :, lanes].reshape(count * rows, part)
+        term = t_mul(left_tokens[...], tokens)
+        for owner in range(4):
+            d_part[owner, :, lanes] = term[
+                owner * down_rows : (owner + 1) * down_rows
+            ].astype(BF16)
+    for y in (other_y, mine_y):
+        send(
+            d_part.at[2 * y + 1 - place.c],
+            d_core.at[y],
+            dc_send.at[y],
+            dc_recv.at[y],
+            place.flip_c(),
+        )
+    r_dh.along(order[depth - 1])
+    r_dh.finish()
+    for y in (other_y, mine_y):
+        landed(d_core.at[y], dc_recv.at[y])
+        add_into(d_core.at[y], d_part.at[2 * y + place.c], down_rows)
+        if y is other_y:
+            send(d_core.at[y], d_y.at[0], dy_send.at[0], dy_recv.at[0], place.flip_y())
+
+    after = middle[...]
+    inv_two = lax.rsqrt(jnp.mean(after * after, axis=-1, keepdims=True) + EPSILON)
+    normed = after * inv_two
+    d_hidden = dh_sum[...]
+    gain_two[...] = jnp.broadcast_to(
+        jnp.sum(d_hidden * normed, axis=0, keepdims=True), gain_two.shape
+    )
+    scaled = d_hidden * vectors[4:5]
+    total = cotangent[...].astype(F32) + inv_two * (
+        scaled - normed * jnp.mean(scaled * normed, axis=-1, keepdims=True)
+    )
+    d_middle[...] = total
+    d_branch[...] = total.astype(BF16)
+    for zi in range(depth):
+        term = mul_t(d_branch[...], o_all[zi].reshape(part, model)).astype(BF16)
+        for piece in range(part // HEAD_DIM):
+            h = zi * (part // HEAD_DIM) + piece
+            at = (h % GROUP) * rows
+            d_mixed[h // GROUP, at : at + rows, :] = term[
+                :, piece * HEAD_DIM : (piece + 1) * HEAD_DIM
+            ]
+    for step in range(depth):
+        r_out.along(order[step])
+        for to in range(step * count // depth, (step + 1) * count // depth):
+            wide_across(to)
+    r_out.finish()
+    layer_out[...] = (middle[...] + out_sum[...]).astype(BF16)
+    landed(d_y.at[0], dy_recv.at[0])
+    down_out[...] = d_y[0].astype(F32) + d_core[mine_y].astype(F32)
+    r_dh.settle()
+    r_out.settle()
+    for copy in sent:
+        copy.wait_send()
+
+
+def call_middle(
+    depth, collective_id, dh, out, hidden, cot, act, d_gate, d_up, o_all, middle, cotangent, vectors
+):
+    count = 2 * depth
+    rows, model = middle.shape
+    units = act.shape[1]
+    wide_rows, down_rows = model // (4 * count), units // 4
+    any_, vmem = pl.BlockSpec(memory_space=pl.ANY), pl.BlockSpec(memory_space=pltpu.VMEM)
+    buffers, sems = Reduce.scratch(depth, False, (rows, model))
+    scratch = [pltpu.VMEM((depth, rows, model), BF16)] * 2
+    scratch += [pltpu.VMEM((rows, model), F32)] * 2
+    scratch += [
+        pltpu.VMEM((depth, 2, rows, model), BF16),
+        pltpu.VMEM((count * rows, units), BF16),
+        pltpu.VMEM((count * rows, units), BF16),
+        pltpu.VMEM((2, count, 2, 2, wide_rows, units), BF16),
+        pltpu.VMEM((2, count, 2, wide_rows, units), BF16),
+        pltpu.VMEM((count, 2, wide_rows, units), BF16),
+        pltpu.VMEM((4, down_rows, model), BF16),
+        pltpu.VMEM((2, down_rows, model), BF16),
+        pltpu.VMEM((1, down_rows, model), BF16),
+        pltpu.VMEM(o_all.shape, BF16),
+    ]
+    scratch += buffers + sems + buffers + sems
+    scratch += [DMA((6,)), DMA((2 * count,)), DMA((2 * count,)), DMA((count,)), DMA((count,))]
+    scratch += [DMA((2,)), DMA((2,)), DMA((1,)), DMA((1,))]
+    return pl.pallas_call(
+        functools.partial(middle_kernel, depth),
+        out_shape=[
+            jax.ShapeDtypeStruct((rows, model), BF16),
+            jax.ShapeDtypeStruct((rows, model), F32),
+            jax.ShapeDtypeStruct((KV_HEADS, GROUP * rows, HEAD_DIM), BF16),
+            jax.ShapeDtypeStruct((rows, model), BF16),
+            jax.ShapeDtypeStruct((8, model), F32),
+            jax.ShapeDtypeStruct((down_rows, model), F32),
+            jax.ShapeDtypeStruct((count, 2, wide_rows, units), BF16),
+        ],
+        in_specs=[any_] * 8 + [vmem] * 3,
+        out_specs=[vmem] * 7,
+        scratch_shapes=scratch,
+        compiler_params=pltpu.CompilerParams(
+            collective_id=collective_id, has_side_effects=True, vmem_limit_bytes=VMEM_JOINED
+        ),
+    )(dh, out, hidden, cot, act, d_gate, d_up, o_all, middle, cotangent, vectors)
+
+
+def last_kernel(depth, *refs):
+    (kv_own, pack_own, wide) = refs[:3]
+    (queries, mixed, lse, d_mixed, cosine, sine, begin) = refs[3:10]
+    (tokens, d_middle, vectors, gain_two, hidden_one, mixed_low, d_branch) = refs[10:17]
+    (input_grad, q_out, kvs_out, o_out, wide_out) = refs[17:22]
+    (kv_all, weights, d_query, delta, d_lin, d_keys, d_kv, o_part, q_part, kvs_part) = refs[22:32]
+    rest = list(refs[32:])
+
+    def take(number):
+        taken = rest[:number]
+        del rest[:number]
+        return taken
+
+    count = 2 * depth
+    devices = 4 * count
+    rows, model = tokens.shape
+    part = model // depth
+    query_width, key_width = HEADS * HEAD_DIM, KV_HEADS * HEAD_DIM
+    qkv_width = query_width + 2 * key_width
+    model_rows = model // devices
+    share = key_width // devices
+    span = 4 * rows
+    score_scale = HEAD_DIM ** (-0.5)
+    scale = score_scale * LOG2E
+
+    place = Place(depth)
+    greet(place, [(lax.rem(place.s + offset, count), place.f) for offset in range(1, count)])
+
+    def reduce_of(own, out, causal=False):
+        block = own.shape[-2:]
+        buffers, sems = Reduce.scratch(depth, True, block)
+        return Reduce(
+            place,
+            True,
+            block[0],
+            own,
+            out,
+            take(len(buffers)),
+            take(len(sems)),
+            causal=causal,
+        )
+
+    r_kv = reduce_of(d_keys, d_kv, True)
+    r_o = reduce_of(o_part, o_out)
+    r_q = reduce_of(q_part, q_out)
+    r_kvs = reduce_of(kvs_part, kvs_out)
+    load_sem, e_send, e_recv = take(3)
+    order = list(range(depth - 1, -1, -1))
+    sent = []
+
+    def depart(offset):
+        to = lax.rem(place.s + offset, count)
+        copy = remote(
+            wide.at[to], wide_out.at[place.s], e_send.at[offset], e_recv.at[offset], (to, place.f)
+        )
+        copy.start()
+        sent.append(copy)
+
+    kv_load = pltpu.make_async_copy(kv_own, kv_all, load_sem.at[0])
+    kv_load.start()
+    own_wide = pltpu.make_async_copy(wide.at[place.s], wide_out.at[place.s], load_sem.at[1])
+    own_wide.start()
+    for offset in range(2, count, 2):
+        depart(offset)
+    for zi in range(depth):
+        lanes = slice(zi * part, (zi + 1) * part)
+        term = t_mul(mixed_low[:, lanes], d_branch[...]).astype(BF16)
+        o_part[zi] = term.reshape(2, 2, 2, model_rows, model)
+    for k in order:
+        r_o.cores(k)
+    for g in range(KV_HEADS):
+        delta[g] = jnp.broadcast_to(
+            jnp.sum(d_mixed[g].astype(F32) * mixed[g], axis=-1, keepdims=True), delta.shape[1:]
+        )
+    d_query[...] = jnp.zeros_like(d_query)
+    kv_load.wait()
+    r_o.over_second(order[0])
+    first_row = (place.s * 4 + place.f) * rows
+    places = first_row + lax.broadcasted_iota(jnp.int32, (rows, span), 0)
+    offsets = lax.broadcasted_iota(jnp.int32, (rows, span), 1)
+
+    def attend(number, carry):
+        keys_at = number * span + offsets
+        visible = jnp.logical_and(keys_at >= begin[...], keys_at <= places)
+        z, x = lax.div(number, 2), lax.rem(number, 2)
+        block = kv_all.at[z, x]
+        target = d_keys.at[z, x]
+        for g in range(KV_HEADS):
+            lanes = slice(g * HEAD_DIM, (g + 1) * HEAD_DIM)
+            others = slice(key_width + g * HEAD_DIM, key_width + (g + 1) * HEAD_DIM)
+            key = block[:, :, :, lanes].reshape(span, HEAD_DIM)
+            value = block[:, :, :, others].reshape(span, HEAD_DIM)
+            scores = mul_t(queries[g], key)
+            d_probs = mul_t(d_mixed[g], value)
+            probs = jnp.exp2(scores * scale - lse[g][:, :1])
+            probs = jnp.where(
+                visible[None], probs.reshape(GROUP, rows, span), 0.0
+            ).reshape(GROUP * rows, span)
+            d_scores = (probs * (d_probs - delta[g][:, :1])).astype(BF16)
+            d_query[g] += jnp.dot(d_scores, key, preferred_element_type=F32)
+            d_key = t_mul(d_scores, queries[g]).astype(BF16)
+            d_value = t_mul(probs.astype(BF16), d_mixed[g]).astype(BF16)
+            target[:, :, :, lanes] = d_key.reshape(2, 2, rows, HEAD_DIM)
+            target[:, :, :, others] = d_value.reshape(2, 2, rows, HEAD_DIM)
+        return carry
+
+    for step in range(depth):
+        k = order[step]
+        zi = place.z - k
+        low = jnp.maximum(2 * zi, 0)
+        high = jnp.minimum(jnp.maximum(2 * zi + 2, 0), place.s + 1)
+        lax.fori_loop(low, high, attend, 0)
+        if k == 0:
+
+            def clear():
+                d_keys[place.z, 1] = jnp.zeros(d_keys.shape[2:], BF16)
+
+            pl.when(place.x == 0)(clear)
+        r_kv.cores(k)
+        if step >= 1:
+            r_kv.over_second(order[step - 1])
+        if step >= 2:
+            r_kv.over_first(order[step - 2])
+        if step + 1 < depth:
+            r_o.over_second(order[step + 1])
+        if step >= 1:
+            r_o.over_first(order[step - 1])
+        if step == 0:
+            for offset in range(1, count, 2):
+                depart(offset)
+
+    for h in range(HEADS):
+        lanes = slice(h * HEAD_DIM, (h + 1) * HEAD_DIM)
+        at = (h % GROUP) * rows
+        head = d_query[h // GROUP, at : at + rows, :] * score_scale
+        d_lin[:, lanes] = turned(head, cosine[...], -sine[...]).astype(BF16)
+    r_kv.over_second(order[depth - 1])
+    if depth >= 2:
+        r_kv.over_first(order[depth - 2])
+    for step in range(max(depth - 2, 0)):
+        r_kv.along(order[step])
+    for zi in range(depth):
+        lanes = slice(zi * part, (zi + 1) * part)
+        term = t_mul(hidden_one[:, lanes], d_lin[:, :query_width]).astype(BF16)
+        q_part[zi] = term.reshape(2, 2, 2, model_rows, query_width)
+    for k in order:
+        r_q.cores(k)
+    r_kv.over_first(order[depth - 1])
+    r_o.over_first(order[depth - 1])
+    for step in range(max(depth - 2, 0), depth):
+        r_kv.along(order[step])
+    r_kv.finish()
+    for step in range(depth):
+        r_q.over_second(order[step])
+    for step in range(depth):
+        r_o.along(order[step])
+    r_o.finish()
+
+    for g in range(KV_HEADS):
+        lanes = slice(g * HEAD_DIM, (g + 1) * HEAD_DIM)
+        to = slice(query_width + g * HEAD_DIM, query_width + (g + 1) * HEAD_DIM)
+        d_lin[:, to] = turned(d_kv[:, lanes] * score_scale, cosine[...], -sine[...]).astype(BF16)
+    d_lin[:, query_width + key_width :] = d_kv[:, key_width:].astype(BF16)
+    inputs = tokens[...].astype(F32)
+    inv_one = lax.rsqrt(jnp.mean(inputs * inputs, axis=-1, keepdims=True) + EPSILON)
+    normed = inputs * inv_one
+    loads = [
+        pltpu.make_async_copy(pack_own.at[zi], weights.at[zi % 2], load_sem.at[2 + zi])
+        for zi in range(depth)
+    ]
+    for copy in loads[:2]:
+        copy.start()
+    pieces = []
+    for zi in range(depth):
+        lanes = slice(zi * part, (zi + 1) * part)
+        term = t_mul(hidden_one[:, lanes], d_lin[:, query_width:]).astype(BF16)
+        kvs_part[zi, :, :, :, :, : 2 * key_width] = term.reshape(
+            2, 2, 2, model_rows, 2 * key_width
+        )
+        loads[zi].wait()
+        block = weights[zi % 2][:, :, :, :, :qkv_width].reshape(part, qkv_width)
+        pieces.append(mul_t(d_lin[...], block))
+        if zi + 2 < depth:
+            loads[zi + 2].start()
+    d_hidden = jnp.concatenate(pieces, axis=1)
+    for step in range(depth):
+        r_q.over_first(order[step])
+    gain_one = jnp.sum(d_hidden * normed, axis=0, keepdims=True)
+    bias = jnp.sum(d_lin[...].astype(F32), axis=0, keepdims=True)
+    chosen = lax.broadcasted_iota(jnp.int32, (key_width, model), 0)
+    chosen = lax.div(chosen, share) * model_rows + lax.rem(chosen, share)
+    chosen = (lax.broadcasted_iota(jnp.int32, (key_width, model), 1) == chosen).astype(BF16)
+    pair = jnp.concatenate(
+        [
+            bias[:, query_width : query_width + key_width],
+            bias[:, query_width + key_width :],
+            jnp.zeros((6, key_width), F32),
+        ],
+        axis=0,
+    )
+    spread = jnp.dot(pair.astype(BF16), chosen, preferred_element_type=F32)
+    small = jnp.concatenate(
+        [
+            gain_one,
+            bias[:, :query_width],
+            spread[0:2],
+            gain_two[0:1],
+            jnp.zeros((123, model), F32),
+        ],
+        axis=0,
+    ).T.astype(BF16)
+    for zi in range(depth):
+        kvs_part[zi, :, :, :, :, 2 * key_width :] = small[zi * part : (zi + 1) * part].reshape(
+            2, 2, 2, model_rows, 128
+        )
+    for k in order:
+        r_kvs.cores(k)
+    scaled = d_hidden * vectors[0:1]
+    input_grad[...] = d_middle[...] + inv_one * (
+        scaled - normed * jnp.mean(scaled * normed, axis=-1, keepdims=True)
+    )
+    for step in range(depth + 2):
+        if step < depth:
+            r_kvs.over_second(order[step])
+        if 0 <= step - 1 < depth:
+            r_kvs.over_first(order[step - 1])
+        if step < depth:
+            r_q.along(order[step])
+        if 0 <= step - 2 < depth:
+            r_kvs.along(order[step - 2])
+    r_q.finish()
+    r_kvs.finish()
+    for offset in range(1, count):
+        origin = lax.rem(place.s + count - offset, count)
+        block = wide_out.at[origin]
+        remote(block, block, e_send.at[0], e_recv.at[offset], place.flip_c()).wait_recv()
+    own_wide.wait()
+    for job in (r_kv, r_o, r_q, r_kvs):
+        job.settle()
+    for copy in sent:
+        copy.wait_send()
+
+
+def call_last(depth, collective_id, hbm, vmems):
+    kv_all, pack_all, wide = hbm
+    tokens = vmems[7]
+    count = 2 * depth
+    rows, model = tokens.shape
+    model_rows = model // (4 * count)
+    query_width, key_width = HEADS * HEAD_DIM, KV_HEADS * HEAD_DIM
+    heads = (KV_HEADS, GROUP * rows, HEAD_DIM)
+    lead = (depth, 2, 2, 2)
+    small_width = 2 * key_width + 128
+    blocks = [
+        (rows, 2 * key_width),
+        (model_rows, model),
+        (model_rows, query_width),
+        (model_rows, small_width),
+    ]
+    scratch = [
+        pltpu.VMEM(kv_all.shape, BF16),
+        pltpu.VMEM((2,) + pack_all.shape[1:], BF16),
+        pltpu.VMEM(heads, F32),
+        pltpu.VMEM(heads, F32),
+        pltpu.VMEM((rows, query_width + 2 * key_width), BF16),
+        pltpu.VMEM(lead + blocks[0], BF16),
+        pltpu.VMEM(blocks[0], F32),
+    ]
+    scratch += [pltpu.VMEM(lead + block, BF16) for block in blocks[1:]]
+    for block in blocks:
+        buffers, sems = Reduce.scratch(depth, True, block)
+        scratch += buffers + sems
+    scratch += [DMA((2 + depth,)), DMA((count,)), DMA((count,))]
+    any_, vmem = pl.BlockSpec(memory_space=pl.ANY), pl.BlockSpec(memory_space=pltpu.VMEM)
+    return pl.pallas_call(
+        functools.partial(last_kernel, depth),
+        out_shape=[
+            jax.ShapeDtypeStruct((rows, model), F32),
+            jax.ShapeDtypeStruct(blocks[2], F32),
+            jax.ShapeDtypeStruct(blocks[3], F32),
+            jax.ShapeDtypeStruct(blocks[1], F32),
+            jax.ShapeDtypeStruct(wide.shape, BF16),
+        ],
+        in_specs=[any_] * 3 + [vmem] * len(vmems),
+        out_specs=[vmem] * 4 + [any_],
+        scratch_shapes=scratch,
+        compiler_params=pltpu.CompilerParams(
+            collective_id=collective_id, has_side_effects=True, vmem_limit_bytes=VMEM_JOINED
+        ),
+    )(*hbm, *vmems)
+
+
 def begin_of(positions, lengths):
     ends = jnp.cumsum(lengths)
     starts = ends - lengths
@@ -991,7 +1915,7 @@
     return jnp.pad(vector, (0, rows - vector.shape[0]))[:, None]
 
 
-def shards(
+def shards_apart(
     tokens,
     cotangent,
     lengths,
@@ -1186,6 +2110,155 @@
     )
 
 
+def shards_joined(
+    tokens,
+    cotangent,
+    lengths,
+    attn_gain,
+    q_weight,
+    q_bias,
+    k_weight,
+    k_bias,
+    v_weight,
+    v_bias,
+    o_weight,
+    mlp_gain,
+    gate_weight,
+    up_weight,
+    down_weight,
+):
+    seq, fsdp = lax.axis_size("seq"), lax.axis_size("fsdp")
+    devices = seq * fsdp
+    depth = seq // 2
+    rows, model = tokens.shape
+    key_width = KV_HEADS * HEAD_DIM
+    model_rows = q_weight.shape[0]
+    kv_share = k_bias.shape[0]
+    units = gate_weight.shape[1] // seq
+    first_row = lax.axis_index(AXES) * rows
+    positions = first_row + jnp.arange(rows, dtype=jnp.int32)
+    begin = begin_of(positions, lengths)
+    cosine, sine_table = rope_tables(positions - begin, HEAD_DIM)
+    cosine_row = jnp.concatenate([cosine, cosine], axis=1)
+    sine_row = jnp.concatenate([-sine_table, sine_table], axis=1)
+
+    small = jnp.concatenate(
+        [column(v, model_rows) for v in (attn_gain, q_bias, k_bias, v_bias, mlp_gain)]
+        + [jnp.zeros((model_rows, 123), BF16)],
+        axis=1,
+    )
+    pack = jnp.concatenate([q_weight, k_weight, v_weight, small], axis=1)
+    wide = jnp.stack([gate_weight, up_weight]).reshape(2, model_rows, seq, units)
+    wide = wide.transpose(0, 2, 1, 3)
+    begin_column = begin[:, None]
+    (
+        pack_all,
+        o_all,
+        kv_all,
+        cot_all,
+        wide_all,
+        down_all,
+        hidden_all,
+        queries,
+        mixed,
+        lse,
+        middle,
+        hidden_one,
+        mixed_low,
+        vectors,
+    ) = call_head(
+        depth,
+        6,
+        pack,
+        o_weight,
+        cotangent,
+        wide,
+        down_weight,
+        tokens,
+        cosine_row,
+        sine_row,
+        begin_column,
+    )
+    w_gate = wide_all[0].reshape(model, units)
+    w_up = wide_all[1].reshape(model, units)
+    w_down = down_all.reshape(units, model)
+    tokens_all = hidden_all.reshape(seq * rows, model)
+    grads_all = cot_all.reshape(seq * rows, model)
+
+    gate = dot(tokens_all, w_gate)
+    up = dot(tokens_all, w_up)
+    sigma = jax.nn.sigmoid(gate)
+    silu = gate * sigma
+    activated = (silu * up).astype(BF16)
+    d_act = dot_t(grads_all, w_down)
+    d_gate = (d_act * up * sigma * (1.0 + gate * (1.0 - sigma))).astype(BF16)
+    d_up = (d_act * silu).astype(BF16)
+    d_hidden_part = dot_t(d_gate, w_gate) + dot_t(d_up, w_up)
+    out_part = dot(activated, w_down)
+    shape = (depth, 2, rows, model)
+    layer_out, d_middle, d_mixed, d_branch, gain_two_grad, down_grad, wide_part = call_middle(
+        depth,
+        7,
+        d_hidden_part.astype(BF16).reshape(shape),
+        out_part.astype(BF16).reshape(shape),
+        hidden_all,
+        cot_all,
+        activated,
+        d_gate,
+        d_up,
+        o_all,
+        middle,
+        cotangent,
+        vectors,
+    )
+    input_grad, q_grad, kvs_grad, o_grad, wide_grad = call_last(
+        depth,
+        8,
+        (kv_all, pack_all, wide_part),
+        (
+            queries,
+            mixed,
+            lse,
+            d_mixed,
+            cosine_row,
+            sine_row,
+            begin_column,
+            tokens,
+            d_middle,
+            vectors,
+            gain_two_grad,
+            hidden_one,
+            mixed_low,
+            d_branch,
+        ),
+    )
+    wide_grad = wide_grad.transpose(1, 2, 0, 3).reshape(2, model_rows, seq * units).astype(F32)
+    small_grad = kvs_grad[:, 2 * key_width :]
+    return (
+        layer_out,
+        input_grad,
+        small_grad[:, 0],
+        q_grad,
+        small_grad[:, 1],
+        kvs_grad[:, :key_width],
+        small_grad[:kv_share, 2],
+        kvs_grad[:, key_width : 2 * key_width],
+        small_grad[:kv_share, 3],
+        o_grad,
+        small_grad[:, 4],
+        wide_grad[0],
+        wide_grad[1],
+        down_grad,
+    )
+
+
+def shards(*arguments):
+    model_rows, rows = arguments[4].shape[0], arguments[0].shape[0]
+    if model_rows % 16 == 0 and rows % 128 == 0:
+        return shards_joined(*arguments)
+    return shards_apart(*arguments)
+
+
 def solution(mesh):
     matrix, vector = P(AXES, None), P(AXES)
     in_specs = (

time: 729 us -> 558 us (0.77)
  Pallas kernels: 545 us -> 444 us
  matrix products: 83.6 us -> 46.1 us
  local copies, waits for them, and re-layouts: 72.2 us -> 52.1 us
  other arithmetic: 24 us -> 5.93 us
    pallas_call x8 -> x3, Pallas kernels: 545 us -> 444 us  [the longest x1 243 us: call_head(): pl.pallas_call(functools.partial(head_kernel, depth), out_shape=outs, in_...]
    dot_general x5 -> x0, matrix products: 28.3 us -> none  [t_dot(): lax.dot_general(left, right, (((0,), (0,)), ((), ())), preferred_element_...]
    concatenate x3 -> x1, local copies, waits for them, and re-layouts: 20.1 us -> 1.7 us  [shards_joined(): pack = jnp.concatenate([q_weight, k_weight, v_weight, small], axis=1)]
    convert_element_type x4 -> x0, local copies, waits for them, and re-layouts: 12.1 us -> none  [the longest x1 5.66 us: shards(): gate_part = t_dot(hidden_all, d_gate).astype(BF16)]
    dot_general x0 -> x2, local copies, waits for them, and re-layouts: none -> 12 us  [the longest x1 6.01 us: dot(): return jnp.dot(left, right, preferred_element_type=F32)]
    dot_general x5 -> x3, matrix products: 26.5 us -> 21.6 us  [dot_t(): lax.dot_general(left, right, (((1,), (1,)), ((), ())), preferred_element_...]
    dot_general x5 -> x3, matrix products: 28.7 us -> 24.4 us  [dot(): return jnp.dot(left, right, preferred_element_type=F32)]
    slice x20 -> x7, local copies, waits for them, and re-layouts: 15.5 us -> 11.5 us  [the longest x1 5.56 us: shards_joined(): w_up = wide_all[1].reshape(model, units)]
where the time goes in v2:
time: 558 us; the launch traced here: 549 us
  Pallas kernels  444 us (80%)
  local copies, waits for them, and re-layouts  52.1 us (9%)
  matrix products  46.1 us (8%)
  other arithmetic  5.93 us (1%)
    pallas_call x1, Pallas kernels, call_head(): pl.pallas_call(functools.partial(head_kernel, depth), out_shape=outs, in_...  243 us
    pallas_call x1, Pallas kernels, call_last(): pl.pallas_call(functools.partial(last_kernel, depth), out_shape=[jax.Shap...  117 us
    pallas_call x1, Pallas kernels, call_middle(): pl.pallas_call(functools.partial(middle_kernel, depth), out_shape=[jax.Sh...  83.8 us
    dot_general x3, matrix products, dot(): return jnp.dot(left, right, preferred_element_type=F32)  24.4 us
    dot_general x3, matrix products, dot_t(): lax.dot_general(left, right, (((1,), (1,)), ((), ())), preferred_element_...  21.6 us

profile of v2, /device:TPU:0, one launch (start us, length us, event | category | flops | bytes accessed | tf_op | source)
XLA Modules:
  0.0 549.3 jit_solution(10370367548187785744)
XLA Ops:
  6.9 1.7 concatenate.10.refs_0_
  9.7 2.7 stack.9
  12.5 1.5 stack.10
  15.7 243.1 %shard_map.254 = (bf16[4,2,2,2,48,2176]{5,4,3,2,1,0:T(8,128)(2,1)}, bf16[4,2,2,2,48,1536]{5,4,3,2,1,0:T(8,128)(2,1)}, bf16[4,2,2,2,128,512]{5,4,3,2,1,0:T(8,128)...) custom-call(bf16[48,2176]{1,0:T(8,128)(2,1)} %concatenate.10.refs_0_, ...), custom_call_target="tpu_custom_call" | custom-call | tf_op jit(solution)/shard_map/pallas_call | solution.py:1334
  258.8 5.6 %fusion.2 = (bf16[1,8,4,48,1120]{4,3,2,1,0:T(8,128)(2,1)S(1)}, bf16[1,8,4,48,1120]{4,3,2,1,0:T(8,128)(2,1)}) fusion(bf16[2,8,4,48,1120]{4,3,2,1,0:T(8,128)(2,1)} %get-tuple-element.43), kind=kLoop, calls=%fused_computation.26 | loop fusion | bytes 13762560 | tf_op jit(solution)/shard_map/slice | solution.py:2183
  264.3 5.9 %fusion.6 = f32[1024,1120]{0,1:T(8,128)} fusion(bf16[1024,1536]{1,0:T(8,128)(2,1)S(1)} %bitcast.44, bf16[1536,1120]{1,0:T(8,128)(2,1)S(1)} %bitcast.38), kind=kOutput, calls=%fused_computation.30 | convolution fusion | flops 3523215360 | bytes 11173888 | tf_op jit(solution)/shard_map/dot_general | solution.py:1903
  270.2 6.0 %copy.92 = f32[1024,1120]{1,0:T(8,128)} copy(f32[1024,1120]{0,1:T(8,128)} %fusion.6) | data formatting | bytes 9175040 | tf_op jit(solution)/shard_map/dot_general | solution.py:1903
  276.2 11.6 %fusion.5 = (f32[1024,1120]{0,1:T(8,128)}, f32[1024,1120]{0,1:T(8,128)}) fusion(f32[1024,1120]{0,1:T(8,128)} %fusion.6, bf16[1024,1536]{1,0:T(8,128)(2,1)} %bitcast.42, bf16[1120,1536]{1,0:T(8,128)(2,1)} %bitcast.52), kind=kOutput, calls=%fused_computation.29 | convolution fusion | flops 3524362240 | bytes 20348928 | tf_op jit(solution)/shard_map/dot_general | solution.py:1907
  287.8 6.0 %copy.88 = f32[1024,1120]{1,0:T(8,128)} copy(f32[1024,1120]{0,1:T(8,128)} %get-tuple-element.83) | data formatting | bytes 9175040 | tf_op jit(solution)/shard_map/mul | solution.py:2194
  293.8 6.0 %copy.91 = f32[1024,1120]{1,0:T(8,128)} copy(f32[1024,1120]{0,1:T(8,128)} %get-tuple-element.84) | data formatting | bytes 9175040 | tf_op jit(solution)/shard_map/dot_general | solution.py:1907
  299.8 12.7 %multiply_convert_fusion = (bf16[1024,1120]{1,0:T(8,128)(2,1)S(1)}, bf16[1024,1120]{1,0:T(8,128)(2,1)S(1)}, bf16[1024,1120]{1,0:T(8,128)(2,1)S(1)}) fusion(f32[1024,1120]{1,0:T(8,128)} %copy.92, f32[1024,1120]{1,0:T(8,128)} %copy.88, f32[1024,1120]{1,0:T(8,128)} %copy.91, bf16[1024,1536]{1,0:T(8,128)(2,1)} %bitcast.43, bf16[1536,1120]{1,0:T(8,128)(2,1)} %bitcast.40), kind=kOutput, calls=%fused_computation.1 | convolution fusion | flops 3539271680 | bytes 27230208 | tf_op jit(solution)/shard_map/dot_general | solution.py:1903
  312.6 5.8 %convolution_convert_fusion = bf16[1024,1536]{1,0:T(8,128)(2,1)} fusion(bf16[1024,1120]{1,0:T(8,128)(2,1)S(1)} %get-tuple-element.73.refs_4_, bf16[1120,1536]{1,0:T(8,128)(2,1)S(1)} %bitcast.53), kind=kOutput, calls=%fused_computation.6 | convolution fusion | flops 3524788224 | bytes 8880128 | tf_op jit(solution)/shard_map/dot_general | solution.py:1903
  318.4 4.3 fusion.7
  322.7 5.8 %add_convert_fusion = bf16[1024,1536]{1,0:T(8,128)(2,1)} fusion(f32[1024,1536]{1,0:T(8,128)S(1)} %fusion.7, bf16[1024,1120]{1,0:T(8,128)(2,1)S(1)} %get-tuple-element.75.refs_6_, bf16[1536,1120]{1,0:T(8,128)(2,1)S(1)} %bitcast.39), kind=kOutput, calls=%fused_computation | convolution fusion | flops 3526361088 | bytes 15171584 | tf_op jit(solution)/shard_map/dot_general | solution.py:1907
  328.5 83.8 %shard_map.255 = (bf16[128,1536]{1,0:T(8,128)(2,1)}, f32[128,1536]{1,0:T(8,128)}, bf16[2,768,128]{2,1,0:T(8,128)(2,1)}, bf16[128,1536]{1,0:T(8,128)(2,1)}, f32[8...) custom-call(bf16[4,2,128,1536]{3,2,1,0:T(8,128)(2,1)} %bitcast.46, ...), custom_call_target="tpu_custom_call" | custom-call | tf_op jit(solution)/shard_map/pallas_call | solution.py:1556
  412.4 117.1 %shard_map.256 = (f32[128,1536]{1,0:T(8,128)}, f32[48,1536]{1,0:T(8,128)}, f32[48,640]{1,0:T(8,128)}, f32[48,1536]{1,0:T(8,128)}, bf16[8,2,48,1120]{3,2,1,0:T(8,128)(2,1)}) custom-call(bf16[4,2,2,2,128,512]{5,4,3,2,1,0:T(8,128)(2,1)} %get-tuple-element.48.refs_0_, bf16[4,2,2,2,48,2176]{5,4,3,2,1,0:T(8,128)(2,1)} %get-tuple-element.49.refs_1_, ...), custom_call_target="tpu_custom_call" | custom-call | tf_op jit(solution)/shard_map/pallas_call | solution.py:1850
  531.0 1.6 slice_reduce_fusion
  534.1 1.7 convert_bitcast_fusion
  536.6 1.7 squeeze.27
  538.9 1.7 squeeze.26
  540.7 1.8 copy.102
  542.4 2.1 copy.103
  544.5 1.7 copy.104
  546.2 1.7 copy.105
  (42 shorter events, 14.5 us)
Async XLA Ops:
  0.6 11.9 %copy-start.6 = (bf16[48,8960]{1,0:T(8,128)(2,1)S(1)}, bf16[48,8960]{1,0:T(8,128)(2,1)}, u32[]{:S(2)}) copy-start(bf16[48,8960]{1,0:T(8,128)(2,1)} %param.28) | copy-start | bytes 2580484
  258.7 5.6 %copy-start.1 = (bf16[4,2,128,1536]{3,2,1,0:T(8,128)(2,1)S(1)}, bf16[4,2,128,1536]{3,2,1,0:T(8,128)(2,1)}, u32[]{:S(2)}) copy-start(bf16[4,2,128,1536]{3,2,1,0:T(8,128)(2,1)} %get-tuple-element.42.refs_2_) | copy-start | bytes 9437188
  299.8 12.8 %copy-start.7 = (bf16[4,280,1536]{2,1,0:T(8,128)(2,1)S(1)}, bf16[4,280,1536]{2,1,0:T(8,128)(2,1)}, u32[]{:S(2)}) copy-start(bf16[4,280,1536]{2,1,0:T(8,128)(2,1)} %get-tuple-element.41) | copy-start | bytes 10321924
  312.5 5.9 %copy-start.2 = (bf16[1024,1120]{1,0:T(8,128)(2,1)}, bf16[1024,1120]{1,0:T(8,128)(2,1)S(1)}, u32[]{:S(2)}) copy-start(bf16[1024,1120]{1,0:T(8,128)(2,1)S(1)} %get-tuple-element.73.refs_4_) | copy-start | bytes 6881284
  312.6 5.9 %copy-start.3 = (bf16[1024,1120]{1,0:T(8,128)(2,1)}, bf16[1024,1120]{1,0:T(8,128)(2,1)S(1)}, u32[]{:S(2)}) copy-start(bf16[1024,1120]{1,0:T(8,128)(2,1)S(1)} %get-tuple-element.74.refs_5_) | copy-start | bytes 6881284
  312.6 10.2 %copy-start.4 = (bf16[1024,1120]{1,0:T(8,128)(2,1)}, bf16[1024,1120]{1,0:T(8,128)(2,1)S(1)}, u32[]{:S(2)}) copy-start(bf16[1024,1120]{1,0:T(8,128)(2,1)S(1)} %get-tuple-element.75.refs_6_) | copy-start | bytes 6881284
  312.6 5.8 %copy-start = (bf16[1,8,4,48,1120]{4,3,2,1,0:T(8,128)(2,1)S(1)}, bf16[1,8,4,48,1120]{4,3,2,1,0:T(8,128)(2,1)}, u32[]{:S(2)}) copy-start(bf16[1,8,4,48,1120]{4,3,2,1,0:T(8,128)(2,1)} %get-tuple-element.72) | copy-start | bytes 10321924
  538.9 9.0 %copy-start.5 = (f32[280,1536]{1,0:T(8,128)S(1)}, f32[280,1536]{1,0:T(8,128)}, u32[]{:S(2)}) copy-start(f32[280,1536]{1,0:T(8,128)} %get-tuple-element.114) | copy-start | bytes 5160964
